TPU v7x, 256 devices: a whole 4x4x8 slice. The times are simulated.
256 devices in a mesh: ckpt: 16 (over y, z_hi), corpus: 16 (over x, z_lo, core).
Axes of the slice: x: 4, y: 4, z: 8 (z_hi: 4, z_lo: 2; z = z_hi * 2 + z_lo), core: 2. Of those that a mesh axis runs over, the one named last changes fastest.
Arguments:
- activations: bfloat16 [16, 2048, 4096], P('ckpt', 'corpus'), may hold values from -6 to 6
- cotangents: bfloat16 [16, 2048, 4096], P('ckpt', 'corpus'), may hold values from -6 to 6
- adapter_down: bfloat16 [16, 4096, 64], P('ckpt'), may hold values from -0.09375 to 0.09375
- projection: bfloat16 [4096, 64], replicated, may hold values from -0.09375 to 0.09375
- learning_rates: int32 [16], P('ckpt'), may hold values from 1 to 8
- gradient_store: bfloat16 [16, 16384, 4096], P('ckpt', 'corpus'), may hold values from -0.09375 to 0.09375
- example_slot: int32 [16, 16, 1024], P('ckpt', 'corpus'), may hold values from 0 to 1023, each once within a row
- query_of_token: int32 [16, 128], replicated, may hold values from 0 to 15, never falling along the last dimension, each value on 1 to 12 neighbouring positions
Outputs:
- influence: float32 [256, 16384], P('ckpt', 'corpus')
Inputs may be any that keep to these rules, and one draw needn't show every extreme that they name: Each row of example_slot is a permutation of 0 to 1023. Each row of query_of_token never falls and gives every query of the shard 1 to 12 tokens; some query has exactly 12.
All inputs are finite; a program needn't handle non-finite values.
Results may differ from a plain program's by a relative error of at most 0.005.
Values may be sent and summed in bfloat16 or wider, within the bound.
No kernel may reach another device: no remote copies, remote signals or barrier semaphores. Data moves between devices by JAX's collectives and lax.ppermute only.
A program may use at most 64 MiB of HBM per device.

v0:
```python
import jax
import jax.numpy as jnp
from jax import lax
from jax.sharding import PartitionSpec as P

QUERIES = 256


def query_gradients(member_ids, low_in, low_out, per_shard):
    member = (
        member_ids[:, :, None] == jnp.arange(per_shard, dtype=jnp.int32)[None, None, :]
    ).astype(jnp.float32)
    weighted = jnp.einsum("btq,btr->btqr", member, low_in.astype(jnp.float32))
    gradients = jnp.einsum("btqr,btk->bqrk", weighted, low_out.astype(jnp.float32))
    blocks, queries, rank_width, out_width = gradients.shape
    return gradients.reshape(blocks * queries, rank_width * out_width).astype(jnp.bfloat16)


def shards(
    activations,
    cotangents,
    adapter_down,
    projection,
    learning_rates,
    gradient_store,
    example_slot,
    query_of_token,
):
    shard_count = lax.axis_size("corpus")
    shard_index = lax.axis_index("corpus")
    per_shard = QUERIES // shard_count
    low_in = jnp.dot(activations[0], adapter_down[0], preferred_element_type=jnp.float32).astype(
        jnp.bfloat16
    )
    low_out = jnp.dot(cotangents[0], projection, preferred_element_type=jnp.float32).astype(
        jnp.bfloat16
    )
    own_ids = lax.dynamic_slice_in_dim(query_of_token, shard_index, 1, 0)
    local_grads = query_gradients(own_ids, low_in[None], low_out[None], per_shard)
    all_grads = lax.all_gather(local_grads, "corpus", axis=0, tiled=True)
    rows_here = gradient_store.shape[1]
    slot_row = example_slot[0, 0]
    inverse = (
        jnp.zeros((rows_here,), jnp.int32).at[slot_row].set(jnp.arange(rows_here, dtype=jnp.int32))
    )
    rate_weight = learning_rates[0].astype(jnp.float32)
    store_rows = gradient_store[0]
    scores = lax.dot_general(
        all_grads, store_rows, (((1,), (1,)), ((), ())), preferred_element_type=jnp.float32
    )
    summed = lax.psum_scatter(
        rate_weight * jnp.take(scores, inverse, axis=1), "ckpt", scatter_dimension=0, tiled=True
    )
    return summed / lax.axis_size("ckpt")


def solution(mesh):
    return jax.shard_map(
        shards,
        mesh=mesh,
        in_specs=(
            P("ckpt", "corpus", None),
            P("ckpt", "corpus", None),
            P("ckpt", None, None),
            P(),
            P("ckpt"),
            P("ckpt", "corpus", None),
            P("ckpt", "corpus", None),
            P(),
        ),
        out_specs=P("ckpt", "corpus"),
        check_vma=False,
    )
```

profile of v0, /device:TPU:8, one launch (start us, length us, event | category | flops | bytes accessed | tf_op | source)
XLA Modules:
  0.0 157.0 jit_solution(4261151992977528558)
XLA Ops:
  6.5 0.0 copy-start
  6.5 0.0 all-gather.2.cloned.1.call-start
  6.5 0.8 dynamic-slice_bitcast_fusion
  7.3 1.8 %fusion.2 = f32[128,64]{0,1:T(8,128)S(1)} fusion(bf16[1,128,4096]{2,1,0:T(8,128)(2,1)} %param.8, bf16[1,4096,64]{1,2,0:T(8,128)(2,1)} %param.10), kind=kOutput, calls=%fused_computation.7 | convolution fusion | flops 67125248 | bytes 1605632 | tf_op jit(solution)/shard_map/dot_general | solution.py:32
  9.2 0.0 copy-done
  9.2 1.8 %convolution_convert_fusion = bf16[16,64,64]{2,1,0:T(8,128)(2,1)S(1)} fusion(bf16[4096,64]{0,1:T(8,128)(2,1)} %param.11, bf16[1,128,4096]{2,1,0:T(8,128)(2,1)S(1)} %copy-done, f32[128,64]{0,1:T(8,128)S(1)} %fusion.2, f32[128,16]{0,1:T(8,128)S(1)} %fusion.12), kind=kOutput, calls=%fused_computation.4 | convolution fusion | flops 84090880 | bytes 1744896 | tf_op jit(solution)/shard_map/btqr,btk->bqrk/dot_general | solution.py:14
  11.0 1.0 convert_element_type.26
  12.0 0.0 all-gather.2.cloned.1.call-update
  12.0 0.0 reduce-scatter.4.cloned.1.call-start
  12.7 0.7 compare_select_fusion
  13.4 4.3 %scatter_custom_fusion = s32[1024]{0:T(1024)S(1)} fusion(s32[1024]{0:T(1024)S(1)} %bitcast.29, s32[1024]{0:T(1024)S(1)} %iota.12, s32[]{:T(128)} %constant.8.clone.1), kind=kCustom, calls=%fused_computation.23 | custom fusion | bytes 4100 | tf_op jit(solution)/shard_map/scatter | solution.py:44
  17.7 33.9 %all-gather.2.cloned.1.call-done = bf16[256,4096]{1,0:T(8,128)(2,1)} async-done(((bf16[16,4096]{1,0:T(8,128)(2,1)}), bf16[256,4096]{1,0:T(8,128)(2,1)}) %all-gather.2.cloned.1.call-update) | async-done | bytes 2097168 | tf_op jit(solution)/shard_map/all_gather | solution.py:40
  51.6 6.4 %fusion = f32[256,1024]{0,1:T(8,128)S(1)} fusion(bf16[256,4096]{1,0:T(8,128)(2,1)} %all-gather.2.cloned.1.call-done, bf16[1,1024,4096]{2,1,0:T(8,128)(2,1)} %param.13), kind=kOutput, calls=%fused_computation.2 | convolution fusion | flops 2147483648 | bytes 11534336 | tf_op jit(solution)/shard_map/dot_general | solution.py:48
  58.0 3.5 %gather_fusion = f32[1024,256]{1,0:T(8,128)S(1)} fusion(f32[256,1024]{0,1:T(8,128)S(1)} %fusion, s32[1024]{0:T(1024)S(1)} %fusion.13), kind=kCustom, calls=%fused_computation | custom fusion | bytes 2101248 | tf_op jit(solution)/shard_map/jit(_take)/gather | solution.py:52
  61.5 0.2 multiply_bitcast_fusion
  61.7 1.3 copy.18
  63.0 0.0 reduce-scatter.4.cloned.1.call-update
  63.1 85.6 %reduce-scatter.4.cloned.1.call-done = f32[16,1024]{1,0:T(8,128)} async-done(((f32[256,1024]{1,0:T(8,128)}), f32[16,1024]{1,0:T(8,128)}) %reduce-scatter.4.cloned.1.call-update) | async-done | bytes 65552 | tf_op jit(solution)/shard_map/reduce_scatter | solution.py:51
  148.7 1.5 broadcast_multiply_fusion
  (4 shorter events, 0.0 us)
Async XLA Ops:
  6.5 2.6 %copy-start = (bf16[1,128,4096]{2,1,0:T(8,128)(2,1)S(1)}, bf16[1,128,4096]{2,1,0:T(8,128)(2,1)}, u32[]{:S(2)}) copy-start(bf16[1,128,4096]{2,1,0:T(8,128)(2,1)} %param.9) | copy-start | bytes 3145732
  6.5 45.1 %all-gather.2.cloned.1.call-start = ((), (), s32[]{:S(2)}) async-start(), calls=%async_computation.1 | async-start | bytes 2228224 | tf_op jit(solution)/shard_map/all_gather | solution.py:40
  12.0 136.7 %reduce-scatter.4.cloned.1.call-start = ((), (), s32[]{:S(2)}) async-start(), calls=%async_computation.2 | async-start | bytes 1114112 | tf_op jit(solution)/shard_map/reduce_scatter | solution.py:51
Sparse Core Ops, SparseCore 0:
  12.1 39.4 all-gather.1
  63.2 85.4 reduce-scatter.3
where the time goes:
time: 158 us; the launch traced here: 157 us
  waiting for transfers between devices  120 us (76%)
  between operations  14.1 us (9%)
  local copies, waits for them, and re-layouts  10.8 us (7%)
  matrix products  10.1 us (6%)
  other arithmetic  2.4 us (2%)
    reduce_scatter x1, waiting for transfers between devices, shards(): lax.psum_scatter(rate_weight * jnp.take(scores, inverse, axis=1), 'ckpt',...  85.6 us
    all_gather x1, waiting for transfers between devices, shards(): all_grads = lax.all_gather(local_grads, 'corpus', axis=0, tiled=True)  33.9 us
    dot_general x1, matrix products, shards(): lax.dot_general(all_grads, store_rows, (((1,), (1,)), ((), ())), preferre...  6.38 us
    scatter x1, local copies, waits for them, and re-layouts, shards(): jnp.zeros((rows_here,), jnp.int32).at[slot_row]  4.31 us
    gather x1, local copies, waits for them, and re-layouts, shards(): jnp.take(scores, inverse, axis=1)  3.47 us
  transfers between devices with their start and end apart: 2, of which 2 were waited for; matrix products, arithmetic and copies ran while one was open for 3% of the time, Pallas kernels for 0%

commit v1 on v0

v1 whole, which is shorter than its diff:
```python
import functools

import jax
import jax.numpy as jnp
from jax import lax
from jax.experimental import pallas as pl
from jax.experimental.pallas import tpu as pltpu
from jax.sharding import PartitionSpec as P

BF16 = jnp.bfloat16
F32 = jnp.float32
NT = (((1,), (1,)), ((), ()))
VMEM = pl.BlockSpec(memory_space=pltpu.VMEM)
SMEM = pl.BlockSpec(memory_space=pltpu.SMEM)
MIB = 1 << 20
SIDE = 4


def factors_kernel(act_ref, cot_ref, down_ref, proj_ref, out_ref, both):
    rank = down_ref.shape[1]
    low_in = jnp.dot(act_ref[...], down_ref[...], preferred_element_type=F32)
    low_out = jnp.dot(cot_ref[...], proj_ref[...], preferred_element_type=F32)
    both[...] = jnp.concatenate([low_in, low_out], axis=1).T
    half = rank // 2
    out_ref[0:half, :] = both[pl.ds(0, half, 2), :].astype(BF16)
    out_ref[half:rank, :] = both[pl.ds(1, half, 2), :].astype(BF16)
    out_ref[rank:, :] = both[rank:, :].astype(BF16)


def factors(act, cot, down, proj):
    tokens, rank, width = act.shape[0], down.shape[1], proj.shape[1]
    return pl.pallas_call(
        factors_kernel,
        out_shape=jax.ShapeDtypeStruct((rank + width, tokens), BF16),
        in_specs=[VMEM] * 4,
        out_specs=VMEM,
        scratch_shapes=[pltpu.VMEM((rank + width, tokens), F32)],
        compiler_params=pltpu.CompilerParams(vmem_limit_bytes=16 * MIB),
        name="factors",
    )(act, cot, down, proj)


def scores_kernel(
    rate_ref, slot_ref, ids_ref, mine_ref, other_ref, store_ref, o0, o1, o2, o3, grads, placed
):
    corpus, ckpt = lax.axis_index("corpus"), lax.axis_index("ckpt")
    x, zlo, core = corpus // 4, (corpus // 2) % 2, corpus % 2
    y, zhi = ckpt // SIDE, ckpt % SIDE
    pieces, depth, tokens = mine_ref.shape
    half = depth // 4
    rows = ids_ref.shape[0]

    def piece(k, ref, flip):
        shard = ((x + SIDE - k // 2) % SIDE) * 4 + (zlo + k % 2) % 2 * 2 + (core + flip) % 2
        at = ((shard // SIDE + SIDE - y) % SIDE) * SIDE + (shard % SIDE + SIDE - zhi) % SIDE
        base = pl.multiple_of(at * rows, rows)
        member = ids_ref[pl.ds(shard, 1), :] == lax.broadcasted_iota(
            jnp.int32, (rows, tokens), 0
        )
        block = ref[k]
        low = block[: 2 * half].astype(F32)
        weights = [
            jnp.where(member[None], low[h * half : (h + 1) * half, None, :], 0.0)
            .astype(BF16)
            .reshape(half * rows, tokens)
            for h in range(2)
        ]
        left = jnp.concatenate(weights, axis=1)
        low_out = block[2 * half :]
        blank = jnp.zeros_like(low_out)
        right = jnp.concatenate(
            [
                jnp.concatenate([low_out, blank], axis=1),
                jnp.concatenate([blank, low_out], axis=1),
            ],
            axis=0,
        )
        product = lax.dot_general(left, right, NT, preferred_element_type=F32).astype(BF16)
        lanes = product.shape[1]
        for p in range(half):
            grads[pl.ds(base, rows), p * lanes : (p + 1) * lanes] = product[
                p * rows : (p + 1) * rows
            ]

    for ref, flip in ((mine_ref, 0), (other_ref, 1)):
        @pl.loop(0, pieces)
        def _(k):
            piece(k, ref, flip)

    examples = store_ref.shape[0]
    chunk = 256
    weight = rate_ref[0].astype(F32) * (1.0 / lax.axis_size("ckpt"))

    @pl.loop(0, examples // chunk)
    def _(c):
        at = pl.multiple_of(c * chunk, chunk)
        part = lax.dot_general(
            grads[...], store_ref[pl.ds(at, chunk), :], NT, preferred_element_type=F32
        )
        placed[:, pl.ds(at, chunk)] = (part * weight).astype(BF16)

    slot = slot_ref[...]
    for c in range(examples // chunk):
        column = lax.broadcasted_iota(jnp.int32, (chunk, examples), 0) + c * chunk
        choose = jnp.where(column == slot, 1.0, 0.0).astype(BF16)
        moved = lax.dot_general(placed[...], choose, NT, preferred_element_type=F32).astype(BF16)
        quarter = moved.shape[0] // SIDE
        for k, out in enumerate((o0, o1, o2, o3)):
            out[:, c * chunk : (c + 1) * chunk] = moved[k * quarter : (k + 1) * quarter]


def scores(rate, slot, ids, mine, other, store):
    shards, per_shard = ids.shape[0], 16
    queries, examples = shards * per_shard, store.shape[0]
    return pl.pallas_call(
        scores_kernel,
        out_shape=[jax.ShapeDtypeStruct((queries // SIDE, examples), BF16)] * SIDE,
        in_specs=[SMEM] + [VMEM] * 5,
        out_specs=[VMEM] * SIDE,
        scratch_shapes=[
            pltpu.VMEM((queries, store.shape[1]), BF16),
            pltpu.VMEM((queries, examples), BF16),
        ],
        compiler_params=pltpu.CompilerParams(vmem_limit_bytes=32 * MIB),
        name="scores",
    )(rate, slot, ids, mine, other, store)


def add_kernel(a, b, c, d, *outs):
    total = (a[...].astype(F32) + b[...].astype(F32)) + (c[...].astype(F32) + d[...].astype(F32))
    rows = outs[0].shape[0]
    for k, out in enumerate(outs):
        out[...] = total[k * rows : (k + 1) * rows].astype(out.dtype)


def add(parts, outs, dtype):
    rows, columns = parts[0].shape
    return pl.pallas_call(
        add_kernel,
        out_shape=[jax.ShapeDtypeStruct((rows // outs, columns), dtype)] * outs,
        in_specs=[VMEM] * SIDE,
        out_specs=[VMEM] * outs,
        name="add",
    )(*parts)


def along(parts, axis, shift):
    n = lax.axis_size(axis)
    return [parts[0]] + [
        lax.ppermute(parts[k], axis, [(i, shift(i, k)) for i in range(n)]) for k in (2, 1, 3)
    ]


def shards(
    activations,
    cotangents,
    adapter_down,
    projection,
    learning_rates,
    gradient_store,
    example_slot,
    query_of_token,
):
    own = factors(activations[0], cotangents[0], adapter_down[0], projection)
    near = lax.ppermute(own, "corpus", [(i, i ^ 2) for i in range(16)])
    pair = jnp.stack([own, near])
    line = [pair] + [
        lax.ppermute(pair, "corpus", [(i, (i + 4 * k) % 16) for i in range(16)]) for k in (1, 2, 3)
    ]
    mine = jnp.concatenate(line)
    other = lax.ppermute(mine, "corpus", [(i, i ^ 1) for i in range(16)])
    store = pltpu.with_memory_space_constraint(gradient_store[0], pltpu.VMEM)
    blocks = scores(learning_rates, example_slot[0], query_of_token, mine, other, store)
    rows = along(blocks, "ckpt", lambda i, k: (i + 4 * k) % 16)
    blocks = add(rows, SIDE, BF16)
    cells = along(blocks, "ckpt", lambda i, k: i // 4 * 4 + (i + k) % 4)
    return add(cells, 1, F32)[0]


def solution(mesh):
    return jax.shard_map(
        shards,
        mesh=mesh,
        in_specs=(
            P("ckpt", "corpus", None),
            P("ckpt", "corpus", None),
            P("ckpt", None, None),
            P(),
            P("ckpt"),
            P("ckpt", "corpus", None),
            P("ckpt", "corpus", None),
            P(),
        ),
        out_specs=P("ckpt", "corpus"),
        check_vma=False,
    )
```

time: 158 us -> 63 us (0.40)
  waiting for transfers between devices: 120 us -> 15.7 us
  starting transfers between devices: 0.04 us -> 22.3 us
  between operations: 14.1 us -> 0.73 us
  Pallas kernels: 0 us -> 11.6 us
  matrix products: 10.1 us -> 0 us
  other arithmetic: 2.4 us -> 0.01 us
    reduce_scatter x1 -> x0, waiting for transfers between devices: 85.6 us -> none  [shards(): lax.psum_scatter(rate_weight * jnp.take(scores, inverse, axis=1), 'ckpt',...]
    all_gather x1 -> x0, waiting for transfers between devices: 33.9 us -> none  [shards(): all_grads = lax.all_gather(local_grads, 'corpus', axis=0, tiled=True)]
    ppermute x0 -> x11, starting transfers between devices: none -> 22.3 us  [the longest x6 14.4 us: along(): lax.ppermute(parts[k], axis, [(i, shift(i, k)) for i in range(n)])]
    ppermute x0 -> x11, waiting for transfers between devices: none -> 15.7 us  [the longest x6 10 us: along(): lax.ppermute(parts[k], axis, [(i, shift(i, k)) for i in range(n)])]
    pallas_call x0 -> x4, Pallas kernels: none -> 11.6 us  [the longest x1 7.51 us: scores(): pl.pallas_call(scores_kernel, out_shape=[jax.ShapeDtypeStruct((queries //...]
    unnamed x3 -> x30, local copies, waits for them, and re-layouts: 1.31 us -> 12.2 us
    dot_general x3 -> x0, matrix products: 10.1 us -> none  [the longest x1 6.38 us: shards(): lax.dot_general(all_grads, store_rows, (((1,), (1,)), ((), ())), preferre...]
    scatter x1 -> x0, local copies, waits for them, and re-layouts: 4.31 us -> none  [shards(): jnp.zeros((rows_here,), jnp.int32).at[slot_row]]
  transfers between devices with their start and end apart: 2 -> 11, of which waited for: 2 -> 8; matrix products, arithmetic and copies ran while one was open for 3% -> 0% of each run, Pallas kernels for 0% -> 0%
where the time goes in v1:
time: 63 us; the launch traced here: 62.5 us
  starting transfers between devices  22.3 us (35%)
  waiting for transfers between devices  15.7 us (25%)
  local copies, waits for them, and re-layouts  12.3 us (20%)
  Pallas kernels  11.6 us (18%)
  between operations  0.73 us (1%)
    ppermute x6, starting transfers between devices, along(): lax.ppermute(parts[k], axis, [(i, shift(i, k)) for i in range(n)])  14.4 us
    unnamed x30, local copies, waits for them, and re-layouts  12.2 us
    ppermute x6, waiting for transfers between devices, along(): lax.ppermute(parts[k], axis, [(i, shift(i, k)) for i in range(n)])  10 us
    pallas_call x1, Pallas kernels, scores(): pl.pallas_call(scores_kernel, out_shape=[jax.ShapeDtypeStruct((queries //...  7.51 us
    ppermute x3, starting transfers between devices, shards(): lax.ppermute(pair, 'corpus', [(i, (i + 4 * k) % 16) for i in range(16)])  5.73 us
    pallas_call x2, Pallas kernels, add(): pl.pallas_call(add_kernel, out_shape=[jax.ShapeDtypeStruct((rows // outs,...  3.23 us
    ppermute x3, waiting for transfers between devices, shards(): lax.ppermute(pair, 'corpus', [(i, (i + 4 * k) % 16) for i in range(16)])  2.79 us
    ppermute x1, starting transfers between devices, shards(): near = lax.ppermute(own, 'corpus', [(i, i ^ 2) for i in range(16)])  2 us
  transfers between devices with their start and end apart: 11, of which 8 were waited for; matrix products, arithmetic and copies ran while one was open for 0% of the time, Pallas kernels for 0%

profile of v1, /device:TPU:8, one launch (start us, length us, event | category | flops | bytes accessed | tf_op | source)
XLA Modules:
  0.0 62.5 jit_solution(11468778832040921847)
XLA Ops:
  0.0 1.5 %copy.9 = bf16[1,4096,64]{2,1,0:T(8,128)(2,1)S(1)} copy(bf16[1,4096,64]{1,2,0:T(8,128)(2,1)} %param.10) | data formatting | bytes 1048576 | tf_op args[2]
  1.5 1.5 %copy.10.proj_ref = bf16[4096,64]{1,0:T(8,128)(2,1)S(1)} copy(bf16[4096,64]{0,1:T(8,128)(2,1)} %param.11) | data formatting | bytes 1048576 | tf_op args[3]
  3.1 1.2 %copy-done.1 = bf16[1,128,4096]{2,1,0:T(8,128)(2,1)S(1)} copy-done((bf16[1,128,4096]{2,1,0:T(8,128)(2,1)S(1)}, bf16[1,128,4096]{2,1,0:T(8,128)(2,1)}, u32[]{:S(2)}) %copy-start.1) | copy-done | bytes 1048600
  4.3 1.2 %copy-done.2 = bf16[1,128,4096]{2,1,0:T(8,128)(2,1)S(1)} copy-done((bf16[1,128,4096]{2,1,0:T(8,128)(2,1)S(1)}, bf16[1,128,4096]{2,1,0:T(8,128)(2,1)}, u32[]{:S(2)}) %copy-start.2) | copy-done | bytes 1048600
  6.3 2.0 %collective-permute-start = (bf16[128,128]{1,0:T(8,128)(2,1)S(1)}, bf16[128,128]{1,0:T(8,128)(2,1)S(1)}, u32[]{:S(2)}, u32[]{:S(2)}) collective-permute-start(bf16[128,128]{1,0:T(8,128)(2,1)S(1)} %factors.1), channel_id=1, source_target_pairs={{0,2},{1,3},{2,0},{3,1},{4,6},{5,7},{6,4},{7,5},{8,10},{9,11},{10,... | collective-permute-start | bytes 98312 | tf_op jit(solution)/shard_map/ppermute | solution.py:165
  8.3 2.0 %collective-permute-done = bf16[128,128]{1,0:T(8,128)(2,1)S(1)} collective-permute-done((bf16[128,128]{1,0:T(8,128)(2,1)S(1)}, bf16[128,128]{1,0:T(8,128)(2,1)S(1)}, u32[]{:S(2)}, u32[]{:S(2)}) %collective-permute-start) | collective-permute-done | bytes 32800 | tf_op jit(solution)/shard_map/ppermute | solution.py:165
  10.3 1.6 %collective-permute-start.1 = (bf16[2,128,128]{2,1,0:T(8,128)(2,1)S(1)}, bf16[2,128,128]{2,1,0:T(8,128)(2,1)S(1)}, u32[]{:S(2)}, u32[]{:S(2)}) collective-permute-start(bf16[2,128,128]{2,1,0:T(8,128)(2,1)S(1)} %pad_maximum_fusion), channel_id=1, source_target_pairs={{0,4},{1,5},{2,6},{3,7},{4,8},{5,9},{6,10},{7,11},{8,12},{9,13},{1... | collective-permute-start | bytes 196616 | tf_op jit(solution)/shard_map/ppermute | solution.py:168
  11.9 2.7 %collective-permute-start.2 = (bf16[2,128,128]{2,1,0:T(8,128)(2,1)S(1)}, bf16[2,128,128]{2,1,0:T(8,128)(2,1)S(1)}, u32[]{:S(2)}, u32[]{:S(2)}) collective-permute-start(bf16[2,128,128]{2,1,0:T(8,128)(2,1)S(1)} %pad_maximum_fusion), channel_id=1, source_target_pairs={{0,8},{1,9},{2,10},{3,11},{4,12},{5,13},{6,14},{7,15},{8,0},{9,1},... | collective-permute-start | bytes 196616 | tf_op jit(solution)/shard_map/ppermute | solution.py:168
  14.6 1.4 %collective-permute-start.3 = (bf16[2,128,128]{2,1,0:T(8,128)(2,1)S(1)}, bf16[2,128,128]{2,1,0:T(8,128)(2,1)S(1)}, u32[]{:S(2)}, u32[]{:S(2)}) collective-permute-start(bf16[2,128,128]{2,1,0:T(8,128)(2,1)S(1)} %pad_maximum_fusion), channel_id=1, source_target_pairs={{0,12},{1,13},{2,14},{3,15},{4,0},{5,1},{6,2},{7,3},{8,4},{9,5},{1... | collective-permute-start | bytes 196616 | tf_op jit(solution)/shard_map/ppermute | solution.py:168
  16.2 1.5 %collective-permute-done.2 = bf16[2,128,128]{2,1,0:T(8,128)(2,1)S(1)} collective-permute-done((bf16[2,128,128]{2,1,0:T(8,128)(2,1)S(1)}, bf16[2,128,128]{2,1,0:T(8,128)(2,1)S(1)}, u32[]{:S(2)}, u32[]{:S(2)}) %collective-permute-start.2) | collective-permute-done | bytes 65568 | tf_op jit(solution)/shard_map/ppermute | solution.py:168
  17.7 1.2 %collective-permute-done.3 = bf16[2,128,128]{2,1,0:T(8,128)(2,1)S(1)} collective-permute-done((bf16[2,128,128]{2,1,0:T(8,128)(2,1)S(1)}, bf16[2,128,128]{2,1,0:T(8,128)(2,1)S(1)}, u32[]{:S(2)}, u32[]{:S(2)}) %collective-permute-start.3) | collective-permute-done | bytes 65568 | tf_op jit(solution)/shard_map/ppermute | solution.py:168
  19.7 0.9 %collective-permute-done.4.other_ref = bf16[8,128,128]{2,1,0:T(8,128)(2,1)S(1)} collective-permute-done((bf16[8,128,128]{2,1,0:T(8,128)(2,1)S(1)}, bf16[8,128,128]{2,1,0:T(8,128)(2,1)S(1)}, u32[]{:S(2)}, u32[]{:S(2)}) %collective-permute-start.4) | collective-permute-done | bytes 262176 | tf_op jit(solution)/shard_map/ppermute | solution.py:171
  20.6 3.4 %copy-done = bf16[1,1024,4096]{2,1,0:T(8,128)(2,1)S(1)} copy-done((bf16[1,1024,4096]{2,1,0:T(8,128)(2,1)S(1)}, bf16[1,1024,4096]{2,1,0:T(8,128)(2,1)}, u32[]{:S(2)}) %copy-start) | copy-done | bytes 8388632
  25.3 7.5 %scores.1 = (bf16[64,1024]{1,0:T(8,128)(2,1)S(1)}, bf16[64,1024]{1,0:T(8,128)(2,1)S(1)}, bf16[64,1024]{1,0:T(8,128)(2,1)S(1)}, bf16[64,1024]{1,0:T(8,128)(2,1)S(1)}) custom-call(s32[1]{0:T(128)S(6)} %copy.15.rate_ref, s32[1,1024]{1,0:T(1,128)S(1)} %bitcast.14, s32[16,128]{1,0:T(8,128)S(1)} %copy-done.4, ...), custom_call_target="tpu_custom_call" | custom-call | tf_op jit(solution)/shard_map/scores/pallas_call | solution.py:115
  33.5 2.3 %collective-permute-start.5 = (bf16[64,1024]{1,0:T(8,128)(2,1)S(1)}, bf16[64,1024]{1,0:T(8,128)(2,1)S(1)}, u32[]{:S(2)}, u32[]{:S(2)}) collective-permute-start(bf16[64,1024]{1,0:T(8,128)(2,1)S(1)} %get-tuple-element.14), channel_id=1, source_target_pairs={{0,128},{16,144},{32,160},{48,176},{64,192},{80,208},{96,224},{112... | collective-permute-start | bytes 393224 | tf_op jit(solution)/shard_map/ppermute | solution.py:150
  35.8 2.0 %collective-permute-start.7 = (bf16[64,1024]{1,0:T(8,128)(2,1)S(1)}, bf16[64,1024]{1,0:T(8,128)(2,1)S(1)}, u32[]{:S(2)}, u32[]{:S(2)}) collective-permute-start(bf16[64,1024]{1,0:T(8,128)(2,1)S(1)} %get-tuple-element.16), channel_id=1, source_target_pairs={{0,192},{16,208},{32,224},{48,240},{64,0},{80,16},{96,32},{112,48}... | collective-permute-start | bytes 393224 | tf_op jit(solution)/shard_map/ppermute | solution.py:150
  37.8 3.5 %collective-permute-done.5.b = bf16[64,1024]{1,0:T(8,128)(2,1)S(1)} collective-permute-done((bf16[64,1024]{1,0:T(8,128)(2,1)S(1)}, bf16[64,1024]{1,0:T(8,128)(2,1)S(1)}, u32[]{:S(2)}, u32[]{:S(2)}) %collective-permute-start.5) | collective-permute-done | bytes 131104 | tf_op jit(solution)/shard_map/ppermute | solution.py:150
  41.3 2.1 %collective-permute-done.6.c = bf16[64,1024]{1,0:T(8,128)(2,1)S(1)} collective-permute-done((bf16[64,1024]{1,0:T(8,128)(2,1)S(1)}, bf16[64,1024]{1,0:T(8,128)(2,1)S(1)}, u32[]{:S(2)}, u32[]{:S(2)}) %collective-permute-start.6) | collective-permute-done | bytes 131104 | tf_op jit(solution)/shard_map/ppermute | solution.py:150
  44.2 1.8 %add.2 = (bf16[16,1024]{1,0:T(8,128)(2,1)}, bf16[16,1024]{1,0:T(8,128)(2,1)}, bf16[16,1024]{1,0:T(8,128)(2,1)}, bf16[16,1024]{1,0:T(8,128)(2,1)}) custom-call(bf16[64,1024]{1,0:T(8,128)(2,1)} %copy-done.3, bf16[64,1024]{1,0:T(8,128)(2,1)} %copy-done.6, bf16[64,1024]{1,0:T(8,128)(2,1)} %copy-done.7, bf16[64,1024]{1,0:T(8,128)(2,1)} %copy-done.8), custom_call_target="tpu_custom_call" | custom-call | tf_op jit(solution)/shard_map/add/pallas_call | solution.py:138
  46.0 6.3 %collective-permute-start.10 = (bf16[16,1024]{1,0:T(8,128)(2,1)}, bf16[16,1024]{1,0:T(8,128)(2,1)S(1)}, u32[]{:S(2)}, u32[]{:S(2)}) collective-permute-start(bf16[16,1024]{1,0:T(8,128)(2,1)} %get-tuple-element.20), channel_id=1, source_target_pairs={{0,48},{16,0},{32,16},{48,32},{64,112},{80,64},{96,80},{112,96},{1... | collective-permute-start | bytes 98312 | tf_op jit(solution)/shard_map/ppermute | solution.py:150
  52.3 0.9 %collective-permute-start.8 = (bf16[16,1024]{1,0:T(8,128)(2,1)}, bf16[16,1024]{1,0:T(8,128)(2,1)S(1)}, u32[]{:S(2)}, u32[]{:S(2)}) collective-permute-start(bf16[16,1024]{1,0:T(8,128)(2,1)} %get-tuple-element.18), channel_id=1, source_target_pairs={{0,32},{16,48},{32,0},{48,16},{64,96},{80,112},{96,64},{112,80},{1... | collective-permute-start | bytes 98312 | tf_op jit(solution)/shard_map/ppermute | solution.py:150
  53.2 2.9 %collective-permute-start.9 = (bf16[16,1024]{1,0:T(8,128)(2,1)}, bf16[16,1024]{1,0:T(8,128)(2,1)S(1)}, u32[]{:S(2)}, u32[]{:S(2)}) collective-permute-start(bf16[16,1024]{1,0:T(8,128)(2,1)} %get-tuple-element.19), channel_id=1, source_target_pairs={{0,16},{16,32},{32,48},{48,0},{64,80},{80,96},{96,112},{112,64},{1... | collective-permute-start | bytes 98312 | tf_op jit(solution)/shard_map/ppermute | solution.py:150
  56.1 4.3 %collective-permute-done.8.b = bf16[16,1024]{1,0:T(8,128)(2,1)S(1)} collective-permute-done((bf16[16,1024]{1,0:T(8,128)(2,1)}, bf16[16,1024]{1,0:T(8,128)(2,1)S(1)}, u32[]{:S(2)}, u32[]{:S(2)}) %collective-permute-start.8) | collective-permute-done | bytes 32800 | tf_op jit(solution)/shard_map/ppermute | solution.py:150
  61.1 1.5 %add.3 = f32[16,1024]{1,0:T(8,128)} custom-call(bf16[16,1024]{1,0:T(8,128)(2,1)} %get-tuple-element.17.a, bf16[16,1024]{1,0:T(8,128)(2,1)} %copy-done.10, bf16[16,1024]{1,0:T(8,128)(2,1)} %copy-done.11, bf16[16,1024]{1,0:T(8,128)(2,1)} %copy-done.9), custom_call_target="tpu_custom_call" | custom-call | tf_op jit(solution)/shard_map/add/pallas_call | solution.py:138
  (34 shorter events, 4.4 us)
Async XLA Ops:
  3.0 1.2 %copy-start.1 = (bf16[1,128,4096]{2,1,0:T(8,128)(2,1)S(1)}, bf16[1,128,4096]{2,1,0:T(8,128)(2,1)}, u32[]{:S(2)}) copy-start(bf16[1,128,4096]{2,1,0:T(8,128)(2,1)} %param.8) | copy-start | bytes 3145732
  4.3 1.2 %copy-start.2 = (bf16[1,128,4096]{2,1,0:T(8,128)(2,1)S(1)}, bf16[1,128,4096]{2,1,0:T(8,128)(2,1)}, u32[]{:S(2)}) copy-start(bf16[1,128,4096]{2,1,0:T(8,128)(2,1)} %param.9) | copy-start | bytes 3145732
  6.3 4.0 %collective-permute-start = (bf16[128,128]{1,0:T(8,128)(2,1)S(1)}, bf16[128,128]{1,0:T(8,128)(2,1)S(1)}, u32[]{:S(2)}, u32[]{:S(2)}) collective-permute-start(bf16[128,128]{1,0:T(8,128)(2,1)S(1)} %factors.1), channel_id=1, source_target_pairs={{0,2},{1,3},{2,0},{3,1},{4,6},{5,7},{6,4},{7,5},{8,10},{9,11},{10,... | collective-permute-start | bytes 98312 | tf_op jit(solution)/shard_map/ppermute | solution.py:165
  10.3 5.8 %collective-permute-start.1 = (bf16[2,128,128]{2,1,0:T(8,128)(2,1)S(1)}, bf16[2,128,128]{2,1,0:T(8,128)(2,1)S(1)}, u32[]{:S(2)}, u32[]{:S(2)}) collective-permute-start(bf16[2,128,128]{2,1,0:T(8,128)(2,1)S(1)} %pad_maximum_fusion), channel_id=1, source_target_pairs={{0,4},{1,5},{2,6},{3,7},{4,8},{5,9},{6,10},{7,11},{8,12},{9,13},{1... | collective-permute-start | bytes 196616 | tf_op jit(solution)/shard_map/ppermute | solution.py:168
  11.9 5.8 %collective-permute-start.2 = (bf16[2,128,128]{2,1,0:T(8,128)(2,1)S(1)}, bf16[2,128,128]{2,1,0:T(8,128)(2,1)S(1)}, u32[]{:S(2)}, u32[]{:S(2)}) collective-permute-start(bf16[2,128,128]{2,1,0:T(8,128)(2,1)S(1)} %pad_maximum_fusion), channel_id=1, source_target_pairs={{0,8},{1,9},{2,10},{3,11},{4,12},{5,13},{6,14},{7,15},{8,0},{9,1},... | collective-permute-start | bytes 196616 | tf_op jit(solution)/shard_map/ppermute | solution.py:168
  14.6 4.3 %collective-permute-start.3 = (bf16[2,128,128]{2,1,0:T(8,128)(2,1)S(1)}, bf16[2,128,128]{2,1,0:T(8,128)(2,1)S(1)}, u32[]{:S(2)}, u32[]{:S(2)}) collective-permute-start(bf16[2,128,128]{2,1,0:T(8,128)(2,1)S(1)} %pad_maximum_fusion), channel_id=1, source_target_pairs={{0,12},{1,13},{2,14},{3,15},{4,0},{5,1},{6,2},{7,3},{8,4},{9,5},{1... | collective-permute-start | bytes 196616 | tf_op jit(solution)/shard_map/ppermute | solution.py:168
  18.9 1.6 %collective-permute-start.4 = (bf16[8,128,128]{2,1,0:T(8,128)(2,1)S(1)}, bf16[8,128,128]{2,1,0:T(8,128)(2,1)S(1)}, u32[]{:S(2)}, u32[]{:S(2)}) collective-permute-start(bf16[8,128,128]{2,1,0:T(8,128)(2,1)S(1)} %constant_dynamic-update-slice_fusion.mine_ref), channel_id=1, source_target_pairs={{0,1},{1,0},{2,3},{3,2},{4,5},{5,4},{6,7},{7,6},{8,9},{9,8},{10,11... | collective-permute-start | bytes 786440 | tf_op jit(solution)/shard_map/ppermute | solution.py:171
  20.6 3.4 %copy-start = (bf16[1,1024,4096]{2,1,0:T(8,128)(2,1)S(1)}, bf16[1,1024,4096]{2,1,0:T(8,128)(2,1)}, u32[]{:S(2)}) copy-start(bf16[1,1024,4096]{2,1,0:T(8,128)(2,1)} %param.13) | copy-start | bytes 25165828
  23.9 0.7 %copy-start.4 = (s32[16,128]{1,0:T(8,128)S(1)}, s32[16,128]{1,0:T(8,128)}, u32[]{:S(2)}) copy-start(s32[16,128]{1,0:T(8,128)} %ids_ref.1) | copy-start | bytes 24580
  24.6 0.7 %copy-start.5 = (s32[1,1,1024]{2,1,0:T(1,128)S(1)}, s32[1,1,1024]{2,1,0:T(1,128)}, u32[]{:S(2)}) copy-start(s32[1,1,1024]{2,1,0:T(1,128)} %param.14) | copy-start | bytes 12292
  32.8 0.6 %copy-start.3 = (bf16[64,1024]{1,0:T(8,128)(2,1)}, bf16[64,1024]{1,0:T(8,128)(2,1)S(1)}, u32[]{:S(2)}) copy-start(bf16[64,1024]{1,0:T(8,128)(2,1)S(1)} %get-tuple-element.13.a) | copy-start | bytes 393220
  33.5 7.8 %collective-permute-start.5 = (bf16[64,1024]{1,0:T(8,128)(2,1)S(1)}, bf16[64,1024]{1,0:T(8,128)(2,1)S(1)}, u32[]{:S(2)}, u32[]{:S(2)}) collective-permute-start(bf16[64,1024]{1,0:T(8,128)(2,1)S(1)} %get-tuple-element.14), channel_id=1, source_target_pairs={{0,128},{16,144},{32,160},{48,176},{64,192},{80,208},{96,224},{112... | collective-permute-start | bytes 393224 | tf_op jit(solution)/shard_map/ppermute | solution.py:150
  35.8 7.7 %collective-permute-start.6 = (bf16[64,1024]{1,0:T(8,128)(2,1)S(1)}, bf16[64,1024]{1,0:T(8,128)(2,1)S(1)}, u32[]{:S(2)}, u32[]{:S(2)}) collective-permute-start(bf16[64,1024]{1,0:T(8,128)(2,1)S(1)} %get-tuple-element.15), channel_id=1, source_target_pairs={{0,64},{16,80},{32,96},{48,112},{64,128},{80,144},{96,160},{112,17... | collective-permute-start | bytes 393224 | tf_op jit(solution)/shard_map/ppermute | solution.py:150
  35.8 7.7 %collective-permute-start.7 = (bf16[64,1024]{1,0:T(8,128)(2,1)S(1)}, bf16[64,1024]{1,0:T(8,128)(2,1)S(1)}, u32[]{:S(2)}, u32[]{:S(2)}) collective-permute-start(bf16[64,1024]{1,0:T(8,128)(2,1)S(1)} %get-tuple-element.16), channel_id=1, source_target_pairs={{0,192},{16,208},{32,224},{48,240},{64,0},{80,16},{96,32},{112,48}... | collective-permute-start | bytes 393224 | tf_op jit(solution)/shard_map/ppermute | solution.py:150
  41.3 2.2 %copy-start.6 = (bf16[64,1024]{1,0:T(8,128)(2,1)}, bf16[64,1024]{1,0:T(8,128)(2,1)S(1)}, u32[]{:S(2)}) copy-start(bf16[64,1024]{1,0:T(8,128)(2,1)S(1)} %collective-permute-done.5.b) | copy-start | bytes 393220
  43.5 0.7 %copy-start.7 = (bf16[64,1024]{1,0:T(8,128)(2,1)}, bf16[64,1024]{1,0:T(8,128)(2,1)S(1)}, u32[]{:S(2)}) copy-start(bf16[64,1024]{1,0:T(8,128)(2,1)S(1)} %collective-permute-done.6.c) | copy-start | bytes 393220
  43.5 0.7 %copy-start.8 = (bf16[64,1024]{1,0:T(8,128)(2,1)}, bf16[64,1024]{1,0:T(8,128)(2,1)S(1)}, u32[]{:S(2)}) copy-start(bf16[64,1024]{1,0:T(8,128)(2,1)S(1)} %collective-permute-done.7.d) | copy-start | bytes 393220
  46.0 10.1 %collective-permute-start.10 = (bf16[16,1024]{1,0:T(8,128)(2,1)}, bf16[16,1024]{1,0:T(8,128)(2,1)S(1)}, u32[]{:S(2)}, u32[]{:S(2)}) collective-permute-start(bf16[16,1024]{1,0:T(8,128)(2,1)} %get-tuple-element.20), channel_id=1, source_target_pairs={{0,48},{16,0},{32,16},{48,32},{64,112},{80,64},{96,80},{112,96},{1... | collective-permute-start | bytes 98312 | tf_op jit(solution)/shard_map/ppermute | solution.py:150
  52.3 8.2 %collective-permute-start.8 = (bf16[16,1024]{1,0:T(8,128)(2,1)}, bf16[16,1024]{1,0:T(8,128)(2,1)S(1)}, u32[]{:S(2)}, u32[]{:S(2)}) collective-permute-start(bf16[16,1024]{1,0:T(8,128)(2,1)} %get-tuple-element.18), channel_id=1, source_target_pairs={{0,32},{16,48},{32,0},{48,16},{64,96},{80,112},{96,64},{112,80},{1... | collective-permute-start | bytes 98312 | tf_op jit(solution)/shard_map/ppermute | solution.py:150
  53.2 7.2 %collective-permute-start.9 = (bf16[16,1024]{1,0:T(8,128)(2,1)}, bf16[16,1024]{1,0:T(8,128)(2,1)S(1)}, u32[]{:S(2)}, u32[]{:S(2)}) collective-permute-start(bf16[16,1024]{1,0:T(8,128)(2,1)} %get-tuple-element.19), channel_id=1, source_target_pairs={{0,16},{16,32},{32,48},{48,0},{64,80},{80,96},{96,112},{112,64},{1... | collective-permute-start | bytes 98312 | tf_op jit(solution)/shard_map/ppermute | solution.py:150
  56.1 4.4 %copy-start.9 = (bf16[16,1024]{1,0:T(8,128)(2,1)}, bf16[16,1024]{1,0:T(8,128)(2,1)S(1)}, u32[]{:S(2)}) copy-start(bf16[16,1024]{1,0:T(8,128)(2,1)S(1)} %collective-permute-done.10.d) | copy-start | bytes 98308
  60.4 0.6 copy-start.10
  60.4 0.6 copy-start.11

commit v2 on v1

v2 whole, which is shorter than its diff:
```python
import jax
import jax.numpy as jnp
from jax import lax
from jax.experimental import pallas as pl
from jax.experimental.pallas import tpu as pltpu
from jax.sharding import PartitionSpec as P

BF16 = jnp.bfloat16
F32 = jnp.float32
NT = (((1,), (1,)), ((), ()))
VMEM = pl.BlockSpec(memory_space=pltpu.VMEM)
SMEM = pl.BlockSpec(memory_space=pltpu.SMEM)
HBM = pl.BlockSpec(memory_space=pltpu.HBM)
MIB = 1 << 20
ANY = pl.BlockSpec(memory_space=pl.ANY)
CUTS = 4
PARTS = 2
ROWS = 16
SIDE = 4
ORDER = (2, 1, 3)
STEPS = (0, 1, 3, 2)


def factors_kernel(act_hbm, cot_hbm, down_hbm, proj_hbm, out_ref, act, cot, down, proj, both, sems):
    pairs = ((act_hbm, act), (down_hbm, down), (cot_hbm, cot), (proj_hbm, proj))
    width = act.shape[1] // CUTS
    copies = [
        [
            pltpu.make_async_copy(
                src.at[:, pl.ds(c * width, width)], dst.at[:, pl.ds(c * width, width)], sems.at[k, c]
            )
            for k, (src, dst) in enumerate(pairs)
        ]
        for c in range(CUTS)
    ]
    for group in copies:
        for copy in group:
            copy.start()
    rank = down.shape[0]
    low_in, low_out = 0.0, 0.0
    for c, group in enumerate(copies):
        for copy in group:
            copy.wait()
        at = slice(c * width, (c + 1) * width)
        low_in += lax.dot_general(down[:, at], act[:, at], NT, preferred_element_type=F32)
        low_out += lax.dot_general(proj[:, at], cot[:, at], NT, preferred_element_type=F32)
    both[...] = low_in
    half = rank // 2
    out_ref[0:half, :] = both[pl.ds(0, half, 2), :].astype(BF16)
    out_ref[half:rank, :] = both[pl.ds(1, half, 2), :].astype(BF16)
    out_ref[rank:, :] = low_out.astype(BF16)


def factors(act, cot, down, proj):
    tokens, rank, width = act.shape[0], down.shape[0], proj.shape[0]
    arrays = [pltpu.with_memory_space_constraint(x, pltpu.HBM) for x in (act, cot, down, proj)]
    return pl.pallas_call(
        factors_kernel,
        out_shape=jax.ShapeDtypeStruct((rank + width, tokens), BF16),
        in_specs=[HBM] * 4,
        out_specs=VMEM,
        scratch_shapes=[pltpu.VMEM(x.shape, BF16) for x in arrays]
        + [pltpu.VMEM((rank, tokens), F32), pltpu.SemaphoreType.DMA((4, CUTS))],
        compiler_params=pltpu.CompilerParams(vmem_limit_bytes=8 * MIB),
        name="factors",
    )(*arrays)


def build(ids_ref, shard, block, rows):
    tokens = block.shape[1]
    half = block.shape[0] // 4
    member = ids_ref[pl.ds(shard, 1), :] == lax.broadcasted_iota(jnp.int32, (rows, tokens), 0)
    low = block[: 2 * half].astype(F32)
    weights = [
        jnp.where(member[None], low[h * half : (h + 1) * half, None, :], 0.0)
        .astype(BF16)
        .reshape(half * rows, tokens)
        for h in range(2)
    ]
    left = jnp.concatenate(weights, axis=1)
    low_out = block[2 * half :]
    blank = jnp.zeros_like(low_out)
    right = jnp.concatenate(
        [
            jnp.concatenate([low_out, blank], axis=1),
            jnp.concatenate([blank, low_out], axis=1),
        ],
        axis=0,
    )
    return lax.dot_general(left, right, NT, preferred_element_type=F32).astype(BF16)


def shard_of(k, flip):
    corpus = lax.axis_index("corpus")
    x, zlo, core = corpus // 4, (corpus // 2) % 2, corpus % 2
    return ((x + SIDE - STEPS[k // 2]) % SIDE) * 4 + (zlo + k % 2) % 2 * 2 + (core + flip) % 2


def row_of(shard, rows):
    ckpt = lax.axis_index("ckpt")
    y, zhi = ckpt // SIDE, ckpt % SIDE
    at = ((shard // SIDE + SIDE - y) % SIDE) * SIDE + (shard % SIDE + SIDE - zhi) % SIDE
    return pl.multiple_of(at * rows, rows)


def choose_kernel(
    rate_ref, slot_hbm, ids_hbm, after_hbm, out_ref, weight_ref, ids_ref, slot_ref, sems
):
    load = pltpu.make_async_copy(slot_hbm, slot_ref, sems.at[0])
    ids_load = pltpu.make_async_copy(ids_hbm, ids_ref, sems.at[1])
    load.start()
    ids_load.start()
    weight_ref[...] = jnp.full(
        weight_ref.shape, rate_ref[0].astype(F32) * (1.0 / lax.axis_size("ckpt")), F32
    )
    load.wait()
    examples = slot_ref.shape[1]
    slot = slot_ref[...]
    step = 128
    for c in range(examples // step):
        column = lax.broadcasted_iota(jnp.int32, (step, examples), 0) + c * step
        out_ref[c * step : (c + 1) * step, :] = jnp.where(column == slot, 1.0, 0.0).astype(BF16)
    ids_load.wait()


def choose(rate, slot, ids, after):
    examples = slot.shape[1]
    return pl.pallas_call(
        choose_kernel,
        out_shape=[
            jax.ShapeDtypeStruct((examples, examples), BF16),
            jax.ShapeDtypeStruct((8, 128), F32),
            jax.ShapeDtypeStruct(ids.shape, ids.dtype),
        ],
        in_specs=[SMEM, HBM, HBM, ANY],
        out_specs=[VMEM] * 3,
        scratch_shapes=[pltpu.VMEM(slot.shape, jnp.int32), pltpu.SemaphoreType.DMA((2,))],
        compiler_params=pltpu.CompilerParams(vmem_limit_bytes=4 * MIB),
        cost_estimate=pl.CostEstimate(flops=10**10, bytes_accessed=2 * MIB, transcendentals=0),
        name="choose",
    )(rate, *(pltpu.with_memory_space_constraint(x, pltpu.HBM) for x in (slot, ids)), after)


def near_kernel(ids_ref, mine_ref, out_ref):
    rows = out_ref.shape[0] // mine_ref.shape[0]
    for k in range(mine_ref.shape[0]):
        product = build(ids_ref, shard_of(k, 0), mine_ref[k], rows)
        lanes = product.shape[1]
        for p in range(product.shape[0] // rows):
            out_ref[k * rows : (k + 1) * rows, p * lanes : (p + 1) * lanes] = product[
                p * rows : (p + 1) * rows
            ]


def near_grads(ids, mine, width):
    queries = mine.shape[0] * ROWS
    return pl.pallas_call(
        near_kernel,
        out_shape=jax.ShapeDtypeStruct((queries, width), BF16),
        in_specs=[VMEM, VMEM],
        out_specs=VMEM,
        compiler_params=pltpu.CompilerParams(vmem_limit_bytes=4 * MIB),
        cost_estimate=pl.CostEstimate(flops=10**9, bytes_accessed=2 * MIB, transcendentals=0),
        name="near_grads",
    )(ids, mine)


def scores_kernel(
    ids_ref, near_ref, other_ref, choose_ref, weight_ref, store_ref, o0, o1, o2, o3,
    grads, placed,
):
    examples = store_ref.shape[0]
    pieces = other_ref.shape[0]
    rows = ROWS
    for k in range(pieces):
        grads[pl.ds(row_of(shard_of(k, 0), rows), rows), :] = near_ref[k * rows : (k + 1) * rows, :]
    for k in range(pieces):
        shard = shard_of(k, 1)
        product = build(ids_ref, shard, other_ref[k], rows)
        base = row_of(shard, rows)
        lanes = product.shape[1]
        for p in range(product.shape[0] // rows):
            grads[pl.ds(base, rows), p * lanes : (p + 1) * lanes] = product[
                p * rows : (p + 1) * rows
            ]

    weight = weight_ref[0:1, 0:1]
    chunk = examples // PARTS
    for c in range(PARTS):
        at = slice(c * chunk, (c + 1) * chunk)
        part = lax.dot_general(grads[...], store_ref[at, :], NT, preferred_element_type=F32)
        placed[:, at] = (part * weight).astype(BF16)

    moved = lax.dot_general(placed[...], choose_ref[...], NT, preferred_element_type=F32)
    moved = moved.astype(BF16)
    quarter = moved.shape[0] // SIDE
    for k, out in enumerate((o0, o1, o2, o3)):
        out[...] = moved[k * quarter : (k + 1) * quarter]


def scores(ids, near, other, chosen, weight, store):
    queries, examples = ids.shape[0] * ROWS, store.shape[0]
    return pl.pallas_call(
        scores_kernel,
        out_shape=[jax.ShapeDtypeStruct((queries // SIDE, examples), BF16)] * SIDE,
        in_specs=[VMEM] * 6,
        out_specs=[VMEM] * SIDE,
        scratch_shapes=[
            pltpu.VMEM((queries, store.shape[1]), BF16),
            pltpu.VMEM((queries, examples), BF16),
        ],
        compiler_params=pltpu.CompilerParams(vmem_limit_bytes=8 * MIB),
        name="scores",
    )(ids, near, other, chosen, weight, store)


def add_kernel(a, b, c, d, *outs):
    total = (a[...].astype(F32) + b[...].astype(F32)) + (c[...].astype(F32) + d[...].astype(F32))
    rows = outs[0].shape[0]
    for k, out in enumerate(outs):
        out[...] = total[k * rows : (k + 1) * rows].astype(out.dtype)


def add(parts, outs, dtype):
    rows, columns = parts[0].shape
    return pl.pallas_call(
        add_kernel,
        out_shape=[jax.ShapeDtypeStruct((rows // outs, columns), dtype)] * outs,
        in_specs=[VMEM] * SIDE,
        out_specs=[VMEM] * outs,
        compiler_params=pltpu.CompilerParams(vmem_limit_bytes=4 * MIB),
        name="add",
    )(*parts)


def along(parts, axis, shift, order=ORDER):
    n = lax.axis_size(axis)
    return [parts[0]] + [
        lax.ppermute(parts[k], axis, [(i, shift(i, k)) for i in range(n)]) for k in order
    ]


def shards(
    activations,
    cotangents,
    adapter_down,
    projection,
    learning_rates,
    gradient_store,
    example_slot,
    query_of_token,
):
    own = factors(activations[0], cotangents[0], adapter_down[0].T, projection.T)
    near = lax.ppermute(own, "corpus", [(i, i ^ 2) for i in range(16)])
    chosen, weight, ids = choose(learning_rates, example_slot[0], query_of_token, own)
    pair = jnp.stack([own, near])
    mine = jnp.concatenate(
        along([pair] * SIDE, "corpus", lambda i, k: (i + 4 * k) % 16, STEPS[1:])
    )
    mine, chosen = lax.optimization_barrier((mine, chosen))
    other = lax.ppermute(mine, "corpus", [(i, i ^ 1) for i in range(16)])
    store = gradient_store[0]
    near_part = near_grads(ids, mine, store.shape[1])
    blocks = scores(ids, near_part, other, chosen, weight, store)
    rows = along(blocks, "ckpt", lambda i, k: (i + 4 * k) % 16)
    blocks = add(rows, SIDE, BF16)
    cells = along(blocks, "ckpt", lambda i, k: i // 4 * 4 + (i + k) % 4)
    return add(cells, 1, F32)[0]


def solution(mesh):
    return jax.shard_map(
        shards,
        mesh=mesh,
        in_specs=(
            P("ckpt", "corpus", None),
            P("ckpt", "corpus", None),
            P("ckpt", None, None),
            P(),
            P("ckpt"),
            P("ckpt", "corpus", None),
            P("ckpt", "corpus", None),
            P(),
        ),
        out_specs=P("ckpt", "corpus"),
        check_vma=False,
    )
```

time: 63 us -> 46.1 us (0.73)
  local copies, waits for them, and re-layouts: 12.3 us -> 0.07 us
  Pallas kernels: 11.6 us -> 8.66 us
  waiting for transfers between devices: 15.7 us -> 13.3 us
  starting transfers between devices: 22.3 us -> 23 us
    unnamed x30 -> x8, local copies, waits for them, and re-layouts: 12.2 us -> 0.05 us
    ppermute x6 -> x9, starting transfers between devices: 14.4 us -> 20.9 us  [along(): lax.ppermute(parts[k], axis, [(i, shift(i, k)) for i in range(n)])]
    ppermute x3 -> x0, starting transfers between devices: 5.73 us -> none  [shards(): lax.ppermute(pair, 'corpus', [(i, (i + 4 * k) % 16) for i in range(16)])]
    pallas_call x1, Pallas kernels: 7.51 us -> 3.62 us  [scores(): pl.pallas_call(scores_kernel, out_shape=[jax.ShapeDtypeStruct((queries //...]
    ppermute x3 -> x0, waiting for transfers between devices: 2.79 us -> none  [shards(): lax.ppermute(pair, 'corpus', [(i, (i + 4 * k) % 16) for i in range(16)])]
    pallas_call x2, Pallas kernels: 3.23 us -> 0.72 us  [add(): pl.pallas_call(add_kernel, out_shape=[jax.ShapeDtypeStruct((rows // outs,...]
    ppermute x6 -> x9, waiting for transfers between devices: 10 us -> 12.4 us  [along(): lax.ppermute(parts[k], axis, [(i, shift(i, k)) for i in range(n)])]
    pallas_call x0 -> x2, Pallas kernels: none -> 1.92 us  [the longest x1 1.22 us: choose(): pl.pallas_call(choose_kernel, out_shape=[jax.ShapeDtypeStruct((examples,...]
  transfers between devices with their start and end apart: 11 -> 11, of which waited for: 8 -> 7; matrix products, arithmetic and copies ran while one was open for 0% -> 0% of each run, Pallas kernels for 0% -> 4%
where the time goes in v2:
time: 46.1 us; the launch traced here: 45.9 us
  starting transfers between devices  23 us (50%)
  waiting for transfers between devices  13.3 us (29%)
  Pallas kernels  8.66 us (19%)
  between operations  0.76 us (2%)
    ppermute x9, starting transfers between devices, along(): lax.ppermute(parts[k], axis, [(i, shift(i, k)) for i in range(n)])  20.9 us
    ppermute x9, waiting for transfers between devices, along(): lax.ppermute(parts[k], axis, [(i, shift(i, k)) for i in range(n)])  12.4 us
    pallas_call x1, Pallas kernels, scores(): pl.pallas_call(scores_kernel, out_shape=[jax.ShapeDtypeStruct((queries //...  3.62 us
    pallas_call x1, Pallas kernels, factors(): pl.pallas_call(factors_kernel, out_shape=jax.ShapeDtypeStruct((rank + wid...  2.39 us
    ppermute x1, starting transfers between devices, shards(): near = lax.ppermute(own, 'corpus', [(i, i ^ 2) for i in range(16)])  2.01 us
    pallas_call x1, Pallas kernels, choose(): pl.pallas_call(choose_kernel, out_shape=[jax.ShapeDtypeStruct((examples,...  1.22 us
  transfers between devices with their start and end apart: 11, of which 7 were waited for; matrix products, arithmetic and copies ran while one was open for 0% of the time, Pallas kernels for 4%

profile of v2, /device:TPU:8, one launch (start us, length us, event | category | flops | bytes accessed | tf_op | source)
XLA Modules:
  0.0 45.9 jit_solution(2241408802929137149)
XLA Ops:
  0.0 2.4 %factors.1.after_hbm = bf16[128,128]{1,0:T(8,128)(2,1)S(1)} custom-call(bf16[128,4096]{1,0:T(8,128)(2,1)} %bitcast.16, bf16[128,4096]{1,0:T(8,128)(2,1)} %bitcast.17, bf16[64,4096]{1,0:T(8,128)(2,1)} %bitcast.18, bf16[64,4096]{1,0:T(8,128)(2,1)} %bitcast.19), custom_call_target="tpu_custom_call" | custom-call | tf_op jit(solution)/shard_map/factors/pallas_call | solution.py:57
  2.4 2.0 %collective-permute-start = (bf16[128,128]{1,0:T(8,128)(2,1)S(1)}, bf16[128,128]{1,0:T(8,128)(2,1)S(1)}, u32[]{:S(2)}, u32[]{:S(2)}) collective-permute-start(bf16[128,128]{1,0:T(8,128)(2,1)S(1)} %factors.1.after_hbm), channel_id=1, source_target_pairs={{0,2},{1,3},{2,0},{3,1},{4,6},{5,7},{6,4},{7,5},{8,10},{9,11},{10,... | collective-permute-start | bytes 98312 | tf_op jit(solution)/shard_map/ppermute | solution.py:254
  5.1 0.0 slice-start
  5.1 1.2 %choose.1 = (bf16[1024,1024]{1,0:T(8,128)(2,1)S(1)}, f32[8,128]{1,0:T(8,128)S(1)}, s32[16,128]{1,0:T(8,128)S(1)}) custom-call(s32[1]{0:T(128)S(6)} %copy.13.rate_ref, s32[1,1024]{1,0:T(1,128)} %bitcast.21, s32[16,128]{1,0:T(8,128)} %ids_hbm.1, bf16[128,128]{1,0:T(8,128)(2,1)S(1)} %factors.1.after_hbm), custom_call_target="tpu_custom_call" | custom-call | flops 10000000000 | bytes 2097152 | tf_op jit(solution)/shard_map/choose/pallas_call | solution.py:128
  6.3 0.1 collective-permute-done
  6.4 3.1 %collective-permute-start.3 = (bf16[2,128,128]{2,1,0:T(8,128)(2,1)S(1)}, bf16[2,128,128]{2,1,0:T(8,128)(2,1)S(1)}, u32[]{:S(2)}, u32[]{:S(2)}) collective-permute-start(bf16[2,128,128]{2,1,0:T(8,128)(2,1)S(1)} %pad_maximum_fusion), channel_id=1, source_target_pairs={{0,8},{1,9},{2,10},{3,11},{4,12},{5,13},{6,14},{7,15},{8,0},{9,1},... | collective-permute-start | bytes 196616 | tf_op jit(solution)/shard_map/ppermute | solution.py:239
  9.5 1.1 %collective-permute-start.2 = (bf16[2,128,128]{2,1,0:T(8,128)(2,1)S(1)}, bf16[2,128,128]{2,1,0:T(8,128)(2,1)S(1)}, u32[]{:S(2)}, u32[]{:S(2)}) collective-permute-start(bf16[2,128,128]{2,1,0:T(8,128)(2,1)S(1)} %pad_maximum_fusion), channel_id=1, source_target_pairs={{0,12},{1,13},{2,14},{3,15},{4,0},{5,1},{6,2},{7,3},{8,4},{9,5},{1... | collective-permute-start | bytes 196616 | tf_op jit(solution)/shard_map/ppermute | solution.py:239
  10.7 0.9 %collective-permute-start.1 = (bf16[2,128,128]{2,1,0:T(8,128)(2,1)S(1)}, bf16[2,128,128]{2,1,0:T(8,128)(2,1)S(1)}, u32[]{:S(2)}, u32[]{:S(2)}) collective-permute-start(bf16[2,128,128]{2,1,0:T(8,128)(2,1)S(1)} %pad_maximum_fusion), channel_id=1, source_target_pairs={{0,4},{1,5},{2,6},{3,7},{4,8},{5,9},{6,10},{7,11},{8,12},{9,13},{1... | collective-permute-start | bytes 196616 | tf_op jit(solution)/shard_map/ppermute | solution.py:239
  11.6 4.6 %collective-permute-done.1 = bf16[2,128,128]{2,1,0:T(8,128)(2,1)S(1)} collective-permute-done((bf16[2,128,128]{2,1,0:T(8,128)(2,1)S(1)}, bf16[2,128,128]{2,1,0:T(8,128)(2,1)S(1)}, u32[]{:S(2)}, u32[]{:S(2)}) %collective-permute-start.1) | collective-permute-done | bytes 65568 | tf_op jit(solution)/shard_map/ppermute | solution.py:239
  16.2 0.1 collective-permute-start.4
  16.3 0.7 %near_grads.1.near_ref = bf16[128,4096]{1,0:T(8,128)(2,1)S(1)} custom-call(s32[16,128]{1,0:T(8,128)S(1)} %get-tuple-element.18.ids_ref, bf16[8,128,128]{2,1,0:T(8,128)(2,1)S(1)} %constant_dynamic-update-slice_fusion.mine_ref), custom_call_target="tpu_custom_call" | custom-call | flops 1000000000 | bytes 2097152 | tf_op jit(solution)/shard_map/near_grads/pallas_call | solution.py:157
  17.0 0.8 %collective-permute-done.4.other_ref = bf16[8,128,128]{2,1,0:T(8,128)(2,1)S(1)} collective-permute-done((bf16[8,128,128]{2,1,0:T(8,128)(2,1)S(1)}, bf16[8,128,128]{2,1,0:T(8,128)(2,1)S(1)}, u32[]{:S(2)}, u32[]{:S(2)}) %collective-permute-start.4) | collective-permute-done | bytes 262176 | tf_op jit(solution)/shard_map/ppermute | solution.py:261
  17.8 3.6 %scores.1 = (bf16[64,1024]{1,0:T(8,128)(2,1)S(1)}, bf16[64,1024]{1,0:T(8,128)(2,1)S(1)}, bf16[64,1024]{1,0:T(8,128)(2,1)S(1)}, bf16[64,1024]{1,0:T(8,128)(2,1)S(1)}) custom-call(s32[16,128]{1,0:T(8,128)S(1)} %get-tuple-element.18.ids_ref, bf16[128,4096]{1,0:T(8,128)(2,1)S(1)} %near_grads.1.near_ref, ...), custom_call_target="tpu_custom_call" | custom-call | tf_op jit(solution)/shard_map/scores/pallas_call | solution.py:203
  21.5 2.4 %collective-permute-start.5 = (bf16[64,1024]{1,0:T(8,128)(2,1)S(1)}, bf16[64,1024]{1,0:T(8,128)(2,1)S(1)}, u32[]{:S(2)}, u32[]{:S(2)}) collective-permute-start(bf16[64,1024]{1,0:T(8,128)(2,1)S(1)} %get-tuple-element.24), channel_id=1, source_target_pairs={{0,128},{16,144},{32,160},{48,176},{64,192},{80,208},{96,224},{112... | collective-permute-start | bytes 393224 | tf_op jit(solution)/shard_map/ppermute | solution.py:239
  23.9 2.0 %collective-permute-start.7 = (bf16[64,1024]{1,0:T(8,128)(2,1)S(1)}, bf16[64,1024]{1,0:T(8,128)(2,1)S(1)}, u32[]{:S(2)}, u32[]{:S(2)}) collective-permute-start(bf16[64,1024]{1,0:T(8,128)(2,1)S(1)} %get-tuple-element.26), channel_id=1, source_target_pairs={{0,192},{16,208},{32,224},{48,240},{64,0},{80,16},{96,32},{112,48}... | collective-permute-start | bytes 393224 | tf_op jit(solution)/shard_map/ppermute | solution.py:239
  25.9 3.5 %collective-permute-done.5.b = bf16[64,1024]{1,0:T(8,128)(2,1)S(1)} collective-permute-done((bf16[64,1024]{1,0:T(8,128)(2,1)S(1)}, bf16[64,1024]{1,0:T(8,128)(2,1)S(1)}, u32[]{:S(2)}, u32[]{:S(2)}) %collective-permute-start.5) | collective-permute-done | bytes 131104 | tf_op jit(solution)/shard_map/ppermute | solution.py:239
  29.4 2.2 %collective-permute-done.6.c = bf16[64,1024]{1,0:T(8,128)(2,1)S(1)} collective-permute-done((bf16[64,1024]{1,0:T(8,128)(2,1)S(1)}, bf16[64,1024]{1,0:T(8,128)(2,1)S(1)}, u32[]{:S(2)}, u32[]{:S(2)}) %collective-permute-start.6) | collective-permute-done | bytes 131104 | tf_op jit(solution)/shard_map/ppermute | solution.py:239
  31.6 0.1 add.2
  31.6 7.3 %collective-permute-start.8 = (bf16[16,1024]{1,0:T(8,128)(2,1)S(1)}, bf16[16,1024]{1,0:T(8,128)(2,1)S(1)}, u32[]{:S(2)}, u32[]{:S(2)}) collective-permute-start(bf16[16,1024]{1,0:T(8,128)(2,1)S(1)} %get-tuple-element.28), channel_id=1, source_target_pairs={{0,32},{16,48},{32,0},{48,16},{64,96},{80,112},{96,64},{112,80},{1... | collective-permute-start | bytes 98312 | tf_op jit(solution)/shard_map/ppermute | solution.py:239
  38.9 1.5 %collective-permute-start.9 = (bf16[16,1024]{1,0:T(8,128)(2,1)S(1)}, bf16[16,1024]{1,0:T(8,128)(2,1)S(1)}, u32[]{:S(2)}, u32[]{:S(2)}) collective-permute-start(bf16[16,1024]{1,0:T(8,128)(2,1)S(1)} %get-tuple-element.29), channel_id=1, source_target_pairs={{0,16},{16,32},{32,48},{48,0},{64,80},{80,96},{96,112},{112,64},{1... | collective-permute-start | bytes 98312 | tf_op jit(solution)/shard_map/ppermute | solution.py:239
  40.4 2.7 %collective-permute-start.10 = (bf16[16,1024]{1,0:T(8,128)(2,1)S(1)}, bf16[16,1024]{1,0:T(8,128)(2,1)S(1)}, u32[]{:S(2)}, u32[]{:S(2)}) collective-permute-start(bf16[16,1024]{1,0:T(8,128)(2,1)S(1)} %get-tuple-element.30), channel_id=1, source_target_pairs={{0,48},{16,0},{32,16},{48,32},{64,112},{80,64},{96,80},{112,96},{1... | collective-permute-start | bytes 98312 | tf_op jit(solution)/shard_map/ppermute | solution.py:239
  43.1 1.9 %collective-permute-done.9.c = bf16[16,1024]{1,0:T(8,128)(2,1)S(1)} collective-permute-done((bf16[16,1024]{1,0:T(8,128)(2,1)S(1)}, bf16[16,1024]{1,0:T(8,128)(2,1)S(1)}, u32[]{:S(2)}, u32[]{:S(2)}) %collective-permute-start.9) | collective-permute-done | bytes 32800 | tf_op jit(solution)/shard_map/ppermute | solution.py:239
  45.0 0.3 collective-permute-done.10.d
  45.2 0.6 %add.3 = f32[16,1024]{1,0:T(8,128)} custom-call(bf16[16,1024]{1,0:T(8,128)(2,1)S(1)} %get-tuple-element.27.a, bf16[16,1024]{1,0:T(8,128)(2,1)S(1)} %collective-permute-done.8.b, bf16[16,1024]{1,0:T(8,128)(2,1)S(1)} %collective-permute-done.9.c, bf16[16,1024]{1,0:T(8,128)(2,1)S(1)} %collective-permute-done.10.d), custom_call_target="tpu_custom_call" | custom-call | tf_op jit(solution)/shard_map/add/pallas_call | solution.py:226
  (15 shorter events, 0.1 us)
Async XLA Ops:
  2.4 4.0 %collective-permute-start = (bf16[128,128]{1,0:T(8,128)(2,1)S(1)}, bf16[128,128]{1,0:T(8,128)(2,1)S(1)}, u32[]{:S(2)}, u32[]{:S(2)}) collective-permute-start(bf16[128,128]{1,0:T(8,128)(2,1)S(1)} %factors.1.after_hbm), channel_id=1, source_target_pairs={{0,2},{1,3},{2,0},{3,1},{4,6},{5,7},{6,4},{7,5},{8,10},{9,11},{10,... | collective-permute-start | bytes 98312 | tf_op jit(solution)/shard_map/ppermute | solution.py:254
  5.1 12.8 %slice-start = ((s8[8388608]{0:T(1024)(128)(4,1)}), s8[4194304]{0:T(1024)(128)(4,1)S(1)}, s32[]{:S(2)}) async-start(s8[8388608]{0:T(1024)(128)(4,1)} %bitcast.12), calls=%async_computation | async-start | bytes 8388608
  5.1 12.8 %slice-start.1 = ((s8[8388608]{0:T(1024)(128)(4,1)}), s8[4194304]{0:T(1024)(128)(4,1)S(1)}, s32[]{:S(2)}) async-start(s8[8388608]{0:T(1024)(128)(4,1)} %bitcast.12), calls=%async_computation.1 | async-start | bytes 8388608
  6.4 9.8 %collective-permute-start.3 = (bf16[2,128,128]{2,1,0:T(8,128)(2,1)S(1)}, bf16[2,128,128]{2,1,0:T(8,128)(2,1)S(1)}, u32[]{:S(2)}, u32[]{:S(2)}) collective-permute-start(bf16[2,128,128]{2,1,0:T(8,128)(2,1)S(1)} %pad_maximum_fusion), channel_id=1, source_target_pairs={{0,8},{1,9},{2,10},{3,11},{4,12},{5,13},{6,14},{7,15},{8,0},{9,1},... | collective-permute-start | bytes 196616 | tf_op jit(solution)/shard_map/ppermute | solution.py:239
  9.5 6.6 %collective-permute-start.2 = (bf16[2,128,128]{2,1,0:T(8,128)(2,1)S(1)}, bf16[2,128,128]{2,1,0:T(8,128)(2,1)S(1)}, u32[]{:S(2)}, u32[]{:S(2)}) collective-permute-start(bf16[2,128,128]{2,1,0:T(8,128)(2,1)S(1)} %pad_maximum_fusion), channel_id=1, source_target_pairs={{0,12},{1,13},{2,14},{3,15},{4,0},{5,1},{6,2},{7,3},{8,4},{9,5},{1... | collective-permute-start | bytes 196616 | tf_op jit(solution)/shard_map/ppermute | solution.py:239
  10.7 5.5 %collective-permute-start.1 = (bf16[2,128,128]{2,1,0:T(8,128)(2,1)S(1)}, bf16[2,128,128]{2,1,0:T(8,128)(2,1)S(1)}, u32[]{:S(2)}, u32[]{:S(2)}) collective-permute-start(bf16[2,128,128]{2,1,0:T(8,128)(2,1)S(1)} %pad_maximum_fusion), channel_id=1, source_target_pairs={{0,4},{1,5},{2,6},{3,7},{4,8},{5,9},{6,10},{7,11},{8,12},{9,13},{1... | collective-permute-start | bytes 196616 | tf_op jit(solution)/shard_map/ppermute | solution.py:239
  16.2 1.6 %collective-permute-start.4 = (bf16[8,128,128]{2,1,0:T(8,128)(2,1)S(1)}, bf16[8,128,128]{2,1,0:T(8,128)(2,1)S(1)}, u32[]{:S(2)}, u32[]{:S(2)}) collective-permute-start(bf16[8,128,128]{2,1,0:T(8,128)(2,1)S(1)} %constant_dynamic-update-slice_fusion.mine_ref), channel_id=1, source_target_pairs={{0,1},{1,0},{2,3},{3,2},{4,5},{5,4},{6,7},{7,6},{8,9},{9,8},{10,11... | collective-permute-start | bytes 786440 | tf_op jit(solution)/shard_map/ppermute | solution.py:261
  21.5 7.9 %collective-permute-start.5 = (bf16[64,1024]{1,0:T(8,128)(2,1)S(1)}, bf16[64,1024]{1,0:T(8,128)(2,1)S(1)}, u32[]{:S(2)}, u32[]{:S(2)}) collective-permute-start(bf16[64,1024]{1,0:T(8,128)(2,1)S(1)} %get-tuple-element.24), channel_id=1, source_target_pairs={{0,128},{16,144},{32,160},{48,176},{64,192},{80,208},{96,224},{112... | collective-permute-start | bytes 393224 | tf_op jit(solution)/shard_map/ppermute | solution.py:239
  23.9 7.7 %collective-permute-start.6 = (bf16[64,1024]{1,0:T(8,128)(2,1)S(1)}, bf16[64,1024]{1,0:T(8,128)(2,1)S(1)}, u32[]{:S(2)}, u32[]{:S(2)}) collective-permute-start(bf16[64,1024]{1,0:T(8,128)(2,1)S(1)} %get-tuple-element.25), channel_id=1, source_target_pairs={{0,64},{16,80},{32,96},{48,112},{64,128},{80,144},{96,160},{112,17... | collective-permute-start | bytes 393224 | tf_op jit(solution)/shard_map/ppermute | solution.py:239
  23.9 7.7 %collective-permute-start.7 = (bf16[64,1024]{1,0:T(8,128)(2,1)S(1)}, bf16[64,1024]{1,0:T(8,128)(2,1)S(1)}, u32[]{:S(2)}, u32[]{:S(2)}) collective-permute-start(bf16[64,1024]{1,0:T(8,128)(2,1)S(1)} %get-tuple-element.26), channel_id=1, source_target_pairs={{0,192},{16,208},{32,224},{48,240},{64,0},{80,16},{96,32},{112,48}... | collective-permute-start | bytes 393224 | tf_op jit(solution)/shard_map/ppermute | solution.py:239
  31.6 11.4 %collective-permute-start.8 = (bf16[16,1024]{1,0:T(8,128)(2,1)S(1)}, bf16[16,1024]{1,0:T(8,128)(2,1)S(1)}, u32[]{:S(2)}, u32[]{:S(2)}) collective-permute-start(bf16[16,1024]{1,0:T(8,128)(2,1)S(1)} %get-tuple-element.28), channel_id=1, source_target_pairs={{0,32},{16,48},{32,0},{48,16},{64,96},{80,112},{96,64},{112,80},{1... | collective-permute-start | bytes 98312 | tf_op jit(solution)/shard_map/ppermute | solution.py:239
  38.9 6.0 %collective-permute-start.9 = (bf16[16,1024]{1,0:T(8,128)(2,1)S(1)}, bf16[16,1024]{1,0:T(8,128)(2,1)S(1)}, u32[]{:S(2)}, u32[]{:S(2)}) collective-permute-start(bf16[16,1024]{1,0:T(8,128)(2,1)S(1)} %get-tuple-element.29), channel_id=1, source_target_pairs={{0,16},{16,32},{32,48},{48,0},{64,80},{80,96},{96,112},{112,64},{1... | collective-permute-start | bytes 98312 | tf_op jit(solution)/shard_map/ppermute | solution.py:239
  40.4 4.8 %collective-permute-start.10 = (bf16[16,1024]{1,0:T(8,128)(2,1)S(1)}, bf16[16,1024]{1,0:T(8,128)(2,1)S(1)}, u32[]{:S(2)}, u32[]{:S(2)}) collective-permute-start(bf16[16,1024]{1,0:T(8,128)(2,1)S(1)} %get-tuple-element.30), channel_id=1, source_target_pairs={{0,48},{16,0},{32,16},{48,32},{64,112},{80,64},{96,80},{112,96},{1... | collective-permute-start | bytes 98312 | tf_op jit(solution)/shard_map/ppermute | solution.py:239

commit v3 on v2

--- a/solution.py
+++ b/solution.py
@@ -1,3 +1,5 @@
+import functools
+
 import jax
 import jax.numpy as jnp
 from jax import lax
@@ -93,13 +95,13 @@
 def shard_of(k, flip):
     corpus = lax.axis_index("corpus")
     x, zlo, core = corpus // 4, (corpus // 2) % 2, corpus % 2
-    return ((x + SIDE - STEPS[k // 2]) % SIDE) * 4 + (zlo + k % 2) % 2 * 2 + (core + flip) % 2
+    return (x ^ STEPS[k // 2]) * 4 + (zlo ^ (k % 2)) * 2 + (core ^ flip)
 
 
 def row_of(shard, rows):
     ckpt = lax.axis_index("ckpt")
     y, zhi = ckpt // SIDE, ckpt % SIDE
-    at = ((shard // SIDE + SIDE - y) % SIDE) * SIDE + (shard % SIDE + SIDE - zhi) % SIDE
+    at = ((shard // SIDE) ^ y) * SIDE + ((shard % SIDE) ^ zhi)
     return pl.multiple_of(at * rows, rows)
 
 
@@ -166,8 +168,8 @@
 
 
 def scores_kernel(
-    ids_ref, near_ref, other_ref, choose_ref, weight_ref, store_ref, o0, o1, o2, o3,
-    grads, placed,
+    ids_ref, near_ref, other_ref, choose_ref, weight_ref, store_ref,
+    home, cross, a1, a3, b1, b3, grads, placed,
 ):
     examples = store_ref.shape[0]
     pieces = other_ref.shape[0]
@@ -193,18 +195,23 @@
 
     moved = lax.dot_general(placed[...], choose_ref[...], NT, preferred_element_type=F32)
     moved = moved.astype(BF16)
-    quarter = moved.shape[0] // SIDE
-    for k, out in enumerate((o0, o1, o2, o3)):
-        out[...] = moved[k * quarter : (k + 1) * quarter]
+    for k, pair in ((0, (home, home)), (2, (cross, cross)), (1, (a1, b1)), (3, (a3, b3))):
+        for first, out in enumerate(pair):
+            for half in range(2):
+                row = (k * SIDE + first + 2 * half) * rows
+                at = out.shape[0] - (4 - 2 * first) * rows if out.shape[0] > 2 * rows else 0
+                at += half * rows
+                out[at : at + rows] = moved[row : row + rows]
 
 
 def scores(ids, near, other, chosen, weight, store):
     queries, examples = ids.shape[0] * ROWS, store.shape[0]
     return pl.pallas_call(
         scores_kernel,
-        out_shape=[jax.ShapeDtypeStruct((queries // SIDE, examples), BF16)] * SIDE,
+        out_shape=[jax.ShapeDtypeStruct((4 * ROWS, examples), BF16)] * 2
+        + [jax.ShapeDtypeStruct((2 * ROWS, examples), BF16)] * 4,
         in_specs=[VMEM] * 6,
-        out_specs=[VMEM] * SIDE,
+        out_specs=[VMEM] * 6,
         scratch_shapes=[
             pltpu.VMEM((queries, store.shape[1]), BF16),
             pltpu.VMEM((queries, examples), BF16),
@@ -214,22 +221,40 @@
     )(ids, near, other, chosen, weight, store)
 
 
-def add_kernel(a, b, c, d, *outs):
-    total = (a[...].astype(F32) + b[...].astype(F32)) + (c[...].astype(F32) + d[...].astype(F32))
-    rows = outs[0].shape[0]
-    for k, out in enumerate(outs):
-        out[...] = total[k * rows : (k + 1) * rows].astype(out.dtype)
-
-
-def add(parts, outs, dtype):
-    rows, columns = parts[0].shape
-    return pl.pallas_call(
-        add_kernel,
-        out_shape=[jax.ShapeDtypeStruct((rows // outs, columns), dtype)] * outs,
+def add_kernel(first, *refs):
+    *parts, a, b = refs
+    rows = a.shape[0]
+    pieces = [x[...] if x.shape[0] == 2 * rows else x[first : first + 2 * rows] for x in parts]
+    one, two, three, four = (x.astype(F32) for x in pieces)
+    total = (one + two) + (three + four)
+    a[...] = total[:rows].astype(a.dtype)
+    b[...] = total[rows:].astype(b.dtype)
+
+
+def add(first, *parts):
+    columns = parts[0].shape[1]
+    return pl.pallas_call(
+        functools.partial(add_kernel, first),
+        out_shape=[jax.ShapeDtypeStruct((ROWS, columns), BF16)] * 2,
         in_specs=[VMEM] * SIDE,
-        out_specs=[VMEM] * outs,
+        out_specs=[VMEM] * 2,
         compiler_params=pltpu.CompilerParams(vmem_limit_bytes=4 * MIB),
         name="add",
+    )(*parts)
+
+
+def total_kernel(a, b, c, d, out):
+    out[...] = (a[...].astype(F32) + b[...].astype(F32)) + (c[...].astype(F32) + d[...].astype(F32))
+
+
+def total(*parts):
+    return pl.pallas_call(
+        total_kernel,
+        out_shape=jax.ShapeDtypeStruct(parts[0].shape, F32),
+        in_specs=[VMEM] * SIDE,
+        out_specs=VMEM,
+        compiler_params=pltpu.CompilerParams(vmem_limit_bytes=4 * MIB),
+        name="total",
     )(*parts)
 
 
@@ -252,20 +277,22 @@
 ):
     own = factors(activations[0], cotangents[0], adapter_down[0].T, projection.T)
     near = lax.ppermute(own, "corpus", [(i, i ^ 2) for i in range(16)])
-    chosen, weight, ids = choose(learning_rates, example_slot[0], query_of_token, own)
     pair = jnp.stack([own, near])
+    chosen, weight, ids = choose(learning_rates, example_slot[0], query_of_token, near)
     mine = jnp.concatenate(
-        along([pair] * SIDE, "corpus", lambda i, k: (i + 4 * k) % 16, STEPS[1:])
+        along([pair] * SIDE, "corpus", lambda i, k: i ^ (4 * k), STEPS[1:])
     )
     mine, chosen = lax.optimization_barrier((mine, chosen))
     other = lax.ppermute(mine, "corpus", [(i, i ^ 1) for i in range(16)])
     store = gradient_store[0]
     near_part = near_grads(ids, mine, store.shape[1])
-    blocks = scores(ids, near_part, other, chosen, weight, store)
-    rows = along(blocks, "ckpt", lambda i, k: (i + 4 * k) % 16)
-    blocks = add(rows, SIDE, BF16)
-    cells = along(blocks, "ckpt", lambda i, k: i // 4 * 4 + (i + k) % 4)
-    return add(cells, 1, F32)[0]
+    home, cross, a1, a3, b1, b3 = scores(ids, near_part, other, chosen, weight, store)
+    over_y = lambda x, k: lax.ppermute(x, "ckpt", [(i, i ^ (4 * k)) for i in range(16)])
+    over_z = lambda x, k: lax.ppermute(x, "ckpt", [(i, i ^ k) for i in range(16)])
+    cross = over_y(cross, 2)
+    mine, two = add(0, home, cross, over_y(a1, 1), over_y(a3, 3))
+    one, three = add(2 * ROWS, home, cross, over_y(b1, 1), over_y(b3, 3))
+    return total(over_z(three, 3), over_z(one, 1), mine, over_z(two, 2))
 
 
 def solution(mesh):

time: 46.1 us -> 43.9 us (0.952)
  waiting for transfers between devices: 13.3 us -> 12 us
  starting transfers between devices: 23 us -> 22.3 us
    ppermute x9 -> x3, starting transfers between devices: 20.9 us -> 4.26 us  [along(): lax.ppermute(parts[k], axis, [(i, shift(i, k)) for i in range(n)])]
    ppermute x0 -> x8, starting transfers between devices: none -> 16 us  [the longest x3 8.95 us: shards(): lax.ppermute(x, 'ckpt', [(i, i ^ k) for i in range(16)])]
    ppermute x9 -> x3, waiting for transfers between devices: 12.4 us -> 3.08 us  [along(): lax.ppermute(parts[k], axis, [(i, shift(i, k)) for i in range(n)])]
    ppermute x0 -> x8, waiting for transfers between devices: none -> 6.75 us  [the longest x3 4.44 us: shards(): lax.ppermute(x, 'ckpt', [(i, i ^ k) for i in range(16)])]
    ppermute x1, waiting for transfers between devices: 0.08 us -> 1.34 us  [shards(): near = lax.ppermute(own, 'corpus', [(i, i ^ 2) for i in range(16)])]
    pallas_call x3 -> x4, Pallas kernels: 4.34 us -> 4.34 us  [the longest x1 3.62 us: scores(): pl.pallas_call(scores_kernel, out_shape=[jax.ShapeDtypeStruct((4 * ROWS,...]
  transfers between devices with their start and end apart: 11 -> 13, of which waited for: 7 -> 7; matrix products, arithmetic and copies ran while one was open for 0% -> 0% of each run, Pallas kernels for 4% -> 5%
where the time goes in v3:
time: 43.9 us; the launch traced here: 43.8 us
  starting transfers between devices  22.3 us (51%)
  waiting for transfers between devices  12 us (27%)
  Pallas kernels  8.65 us (20%)
  between operations  0.74 us (2%)
    ppermute x3, starting transfers between devices, shards(): lax.ppermute(x, 'ckpt', [(i, i ^ k) for i in range(16)])  8.95 us
    ppermute x5, starting transfers between devices, shards(): lax.ppermute(x, 'ckpt', [(i, i ^ 4 * k) for i in range(16)])  7.04 us
    ppermute x3, waiting for transfers between devices, shards(): lax.ppermute(x, 'ckpt', [(i, i ^ k) for i in range(16)])  4.44 us
    ppermute x3, starting transfers between devices, along(): lax.ppermute(parts[k], axis, [(i, shift(i, k)) for i in range(n)])  4.26 us
    pallas_call x1, Pallas kernels, scores(): pl.pallas_call(scores_kernel, out_shape=[jax.ShapeDtypeStruct((4 * ROWS,...  3.62 us
    ppermute x3, waiting for transfers between devices, along(): lax.ppermute(parts[k], axis, [(i, shift(i, k)) for i in range(n)])  3.08 us
    pallas_call x1, Pallas kernels, factors(): pl.pallas_call(factors_kernel, out_shape=jax.ShapeDtypeStruct((rank + wid...  2.39 us
    ppermute x5, waiting for transfers between devices, shards(): lax.ppermute(x, 'ckpt', [(i, i ^ 4 * k) for i in range(16)])  2.32 us
  transfers between devices with their start and end apart: 13, of which 7 were waited for; matrix products, arithmetic and copies ran while one was open for 0% of the time, Pallas kernels for 5%

profile of v3, /device:TPU:8, one launch (start us, length us, event | category | flops | bytes accessed | tf_op | source)
XLA Modules:
  0.0 43.8 jit_solution(16180481671991516663)
XLA Ops:
  0.0 2.4 %factors.1 = bf16[128,128]{1,0:T(8,128)(2,1)S(1)} custom-call(bf16[128,4096]{1,0:T(8,128)(2,1)} %bitcast.17, bf16[128,4096]{1,0:T(8,128)(2,1)} %bitcast.18, bf16[64,4096]{1,0:T(8,128)(2,1)} %bitcast.19, bf16[64,4096]{1,0:T(8,128)(2,1)} %bitcast.20), custom_call_target="tpu_custom_call" | custom-call | tf_op jit(solution)/shard_map/factors/pallas_call | solution.py:59
  2.4 2.0 %collective-permute-start = (bf16[128,128]{1,0:T(8,128)(2,1)S(1)}, bf16[128,128]{1,0:T(8,128)(2,1)S(1)}, u32[]{:S(2)}, u32[]{:S(2)}) collective-permute-start(bf16[128,128]{1,0:T(8,128)(2,1)S(1)} %factors.1), channel_id=1, source_target_pairs={{0,2},{1,3},{2,0},{3,1},{4,6},{5,7},{6,4},{7,5},{8,10},{9,11},{10,... | collective-permute-start | bytes 98312 | tf_op jit(solution)/shard_map/ppermute | solution.py:279
  5.1 1.3 %collective-permute-done.after_hbm = bf16[128,128]{1,0:T(8,128)(2,1)S(1)} collective-permute-done((bf16[128,128]{1,0:T(8,128)(2,1)S(1)}, bf16[128,128]{1,0:T(8,128)(2,1)S(1)}, u32[]{:S(2)}, u32[]{:S(2)}) %collective-permute-start) | collective-permute-done | bytes 32800 | tf_op jit(solution)/shard_map/ppermute | solution.py:279
  6.4 3.1 %collective-permute-start.3 = (bf16[2,128,128]{2,1,0:T(8,128)(2,1)S(1)}, bf16[2,128,128]{2,1,0:T(8,128)(2,1)S(1)}, u32[]{:S(2)}, u32[]{:S(2)}) collective-permute-start(bf16[2,128,128]{2,1,0:T(8,128)(2,1)S(1)} %pad_maximum_fusion), channel_id=1, source_target_pairs={{0,8},{1,9},{2,10},{3,11},{4,12},{5,13},{6,14},{7,15},{8,0},{9,1},... | collective-permute-start | bytes 196616 | tf_op jit(solution)/shard_map/ppermute | solution.py:264
  9.5 1.1 %collective-permute-start.2 = (bf16[2,128,128]{2,1,0:T(8,128)(2,1)S(1)}, bf16[2,128,128]{2,1,0:T(8,128)(2,1)S(1)}, u32[]{:S(2)}, u32[]{:S(2)}) collective-permute-start(bf16[2,128,128]{2,1,0:T(8,128)(2,1)S(1)} %pad_maximum_fusion), channel_id=1, source_target_pairs={{0,12},{1,13},{2,14},{3,15},{4,8},{5,9},{6,10},{7,11},{8,4},{9,5},... | collective-permute-start | bytes 196616 | tf_op jit(solution)/shard_map/ppermute | solution.py:264
  10.7 1.2 %choose.1 = (bf16[1024,1024]{1,0:T(8,128)(2,1)S(1)}, f32[8,128]{1,0:T(8,128)S(1)}, s32[16,128]{1,0:T(8,128)S(1)}) custom-call(s32[1]{0:T(128)S(6)} %copy.13.rate_ref, s32[1,1024]{1,0:T(1,128)} %bitcast.21, s32[16,128]{1,0:T(8,128)} %ids_hbm.1, bf16[128,128]{1,0:T(8,128)(2,1)S(1)} %collective-permute-done.after_hbm), custom_call_target="tpu_custom_call" | custom-call | flops 10000000000 | bytes 2097152 | tf_op jit(solution)/shard_map/choose/pallas_call | solution.py:130
  11.9 3.0 %collective-permute-done.1 = bf16[2,128,128]{2,1,0:T(8,128)(2,1)S(1)} collective-permute-done((bf16[2,128,128]{2,1,0:T(8,128)(2,1)S(1)}, bf16[2,128,128]{2,1,0:T(8,128)(2,1)S(1)}, u32[]{:S(2)}, u32[]{:S(2)}) %collective-permute-start.1) | collective-permute-done | bytes 65568 | tf_op jit(solution)/shard_map/ppermute | solution.py:264
  14.9 0.1 collective-permute-done.2
  15.0 0.1 collective-permute-start.4
  15.1 0.7 %near_grads.1.near_ref = bf16[128,4096]{1,0:T(8,128)(2,1)S(1)} custom-call(s32[16,128]{1,0:T(8,128)S(1)} %get-tuple-element.20.ids_ref, bf16[8,128,128]{2,1,0:T(8,128)(2,1)S(1)} %constant_dynamic-update-slice_fusion.mine_ref), custom_call_target="tpu_custom_call" | custom-call | flops 1000000000 | bytes 2097152 | tf_op jit(solution)/shard_map/near_grads/pallas_call | solution.py:159
  15.9 0.8 %collective-permute-done.4.other_ref = bf16[8,128,128]{2,1,0:T(8,128)(2,1)S(1)} collective-permute-done((bf16[8,128,128]{2,1,0:T(8,128)(2,1)S(1)}, bf16[8,128,128]{2,1,0:T(8,128)(2,1)S(1)}, u32[]{:S(2)}, u32[]{:S(2)}) %collective-permute-start.4) | collective-permute-done | bytes 262176 | tf_op jit(solution)/shard_map/ppermute | solution.py:286
  16.7 3.6 %scores.1 = (bf16[64,1024]{1,0:T(8,128)(2,1)S(1)}, bf16[64,1024]{1,0:T(8,128)(2,1)S(1)}, bf16[32,1024]{1,0:T(8,128)(2,1)S(1)}, bf16[32,1024]{1,0:T(8,128)(2,1)S(...) custom-call(s32[16,128]{1,0:T(8,128)S(1)} %get-tuple-element.20.ids_ref, ...), custom_call_target="tpu_custom_call" | custom-call | tf_op jit(solution)/shard_map/scores/pallas_call | solution.py:209
  20.3 2.4 %collective-permute-start.5 = (bf16[64,1024]{1,0:T(8,128)(2,1)S(1)}, bf16[64,1024]{1,0:T(8,128)(2,1)S(1)}, u32[]{:S(2)}, u32[]{:S(2)}) collective-permute-start(bf16[64,1024]{1,0:T(8,128)(2,1)S(1)} %get-tuple-element.26), channel_id=1, source_target_pairs={{0,128},{16,144},{32,160},{48,176},{64,192},{80,208},{96,224},{112... | collective-permute-start | bytes 393224 | tf_op jit(solution)/shard_map/ppermute | solution.py:290
  22.7 1.3 %collective-permute-start.10 = (bf16[32,1024]{1,0:T(8,128)(2,1)S(1)}, bf16[32,1024]{1,0:T(8,128)(2,1)S(1)}, u32[]{:S(2)}, u32[]{:S(2)}) collective-permute-start(bf16[32,1024]{1,0:T(8,128)(2,1)S(1)} %get-tuple-element.31), channel_id=1, source_target_pairs={{0,64},{16,80},{32,96},{48,112},{64,0},{80,16},{96,32},{112,48},{1... | collective-permute-start | bytes 196616 | tf_op jit(solution)/shard_map/ppermute | solution.py:290
  24.0 0.4 %collective-permute-start.11 = (bf16[32,1024]{1,0:T(8,128)(2,1)S(1)}, bf16[32,1024]{1,0:T(8,128)(2,1)S(1)}, u32[]{:S(2)}, u32[]{:S(2)}) collective-permute-start(bf16[32,1024]{1,0:T(8,128)(2,1)S(1)} %get-tuple-element.32), channel_id=1, source_target_pairs={{0,192},{16,208},{32,224},{48,240},{64,128},{80,144},{96,160},{112... | collective-permute-start | bytes 196616 | tf_op jit(solution)/shard_map/ppermute | solution.py:290
  24.5 0.7 %collective-permute-start.6 = (bf16[32,1024]{1,0:T(8,128)(2,1)S(1)}, bf16[32,1024]{1,0:T(8,128)(2,1)S(1)}, u32[]{:S(2)}, u32[]{:S(2)}) collective-permute-start(bf16[32,1024]{1,0:T(8,128)(2,1)S(1)} %get-tuple-element.27), channel_id=1, source_target_pairs={{0,64},{16,80},{32,96},{48,112},{64,0},{80,16},{96,32},{112,48},{1... | collective-permute-start | bytes 196616 | tf_op jit(solution)/shard_map/ppermute | solution.py:290
  25.1 2.2 %collective-permute-start.7 = (bf16[32,1024]{1,0:T(8,128)(2,1)S(1)}, bf16[32,1024]{1,0:T(8,128)(2,1)S(1)}, u32[]{:S(2)}, u32[]{:S(2)}) collective-permute-start(bf16[32,1024]{1,0:T(8,128)(2,1)S(1)} %get-tuple-element.28), channel_id=1, source_target_pairs={{0,192},{16,208},{32,224},{48,240},{64,128},{80,144},{96,160},{112... | collective-permute-start | bytes 196616 | tf_op jit(solution)/shard_map/ppermute | solution.py:290
  27.3 2.3 %collective-permute-done.10.refs_2_ = bf16[32,1024]{1,0:T(8,128)(2,1)S(1)} collective-permute-done((bf16[32,1024]{1,0:T(8,128)(2,1)S(1)}, bf16[32,1024]{1,0:T(8,128)(2,1)S(1)}, u32[]{:S(2)}, u32[]{:S(2)}) %collective-permute-start.10) | collective-permute-done | bytes 65568 | tf_op jit(solution)/shard_map/ppermute | solution.py:290
  29.7 7.3 %collective-permute-start.12 = (bf16[16,1024]{1,0:T(8,128)(2,1)S(1)}, bf16[16,1024]{1,0:T(8,128)(2,1)S(1)}, u32[]{:S(2)}, u32[]{:S(2)}) collective-permute-start(bf16[16,1024]{1,0:T(8,128)(2,1)S(1)} %get-tuple-element.34), channel_id=1, source_target_pairs={{0,32},{16,48},{32,0},{48,16},{64,96},{80,112},{96,64},{112,80},{1... | collective-permute-start | bytes 98312 | tf_op jit(solution)/shard_map/ppermute | solution.py:291
  37.0 0.1 collective-permute-start.8
  37.1 1.6 %collective-permute-start.9 = (bf16[16,1024]{1,0:T(8,128)(2,1)S(1)}, bf16[16,1024]{1,0:T(8,128)(2,1)S(1)}, u32[]{:S(2)}, u32[]{:S(2)}) collective-permute-start(bf16[16,1024]{1,0:T(8,128)(2,1)S(1)} %get-tuple-element.30), channel_id=1, source_target_pairs={{0,16},{16,0},{32,48},{48,32},{64,80},{80,64},{96,112},{112,96},{1... | collective-permute-start | bytes 98312 | tf_op jit(solution)/shard_map/ppermute | solution.py:291
  38.7 0.2 collective-permute-done.12.d
  38.9 4.3 %collective-permute-done.8.a = bf16[16,1024]{1,0:T(8,128)(2,1)S(1)} collective-permute-done((bf16[16,1024]{1,0:T(8,128)(2,1)S(1)}, bf16[16,1024]{1,0:T(8,128)(2,1)S(1)}, u32[]{:S(2)}, u32[]{:S(2)}) %collective-permute-start.8) | collective-permute-done | bytes 32800 | tf_op jit(solution)/shard_map/ppermute | solution.py:291
  43.1 0.6 %total.1 = f32[16,1024]{1,0:T(8,128)} custom-call(bf16[16,1024]{1,0:T(8,128)(2,1)S(1)} %collective-permute-done.8.a, bf16[16,1024]{1,0:T(8,128)(2,1)S(1)} %collective-permute-done.9.b, bf16[16,1024]{1,0:T(8,128)(2,1)S(1)} %get-tuple-element.33.c, bf16[16,1024]{1,0:T(8,128)(2,1)S(1)} %collective-permute-done.12.d), custom_call_target="tpu_custom_call" | custom-call | tf_op jit(solution)/shard_map/total/pallas_call | solution.py:251
  (20 shorter events, 0.2 us)
Async XLA Ops:
  2.4 4.0 %collective-permute-start = (bf16[128,128]{1,0:T(8,128)(2,1)S(1)}, bf16[128,128]{1,0:T(8,128)(2,1)S(1)}, u32[]{:S(2)}, u32[]{:S(2)}) collective-permute-start(bf16[128,128]{1,0:T(8,128)(2,1)S(1)} %factors.1), channel_id=1, source_target_pairs={{0,2},{1,3},{2,0},{3,1},{4,6},{5,7},{6,4},{7,5},{8,10},{9,11},{10,... | collective-permute-start | bytes 98312 | tf_op jit(solution)/shard_map/ppermute | solution.py:279
  6.4 8.6 %collective-permute-start.3 = (bf16[2,128,128]{2,1,0:T(8,128)(2,1)S(1)}, bf16[2,128,128]{2,1,0:T(8,128)(2,1)S(1)}, u32[]{:S(2)}, u32[]{:S(2)}) collective-permute-start(bf16[2,128,128]{2,1,0:T(8,128)(2,1)S(1)} %pad_maximum_fusion), channel_id=1, source_target_pairs={{0,8},{1,9},{2,10},{3,11},{4,12},{5,13},{6,14},{7,15},{8,0},{9,1},... | collective-permute-start | bytes 196616 | tf_op jit(solution)/shard_map/ppermute | solution.py:264
  9.5 5.5 %collective-permute-start.2 = (bf16[2,128,128]{2,1,0:T(8,128)(2,1)S(1)}, bf16[2,128,128]{2,1,0:T(8,128)(2,1)S(1)}, u32[]{:S(2)}, u32[]{:S(2)}) collective-permute-start(bf16[2,128,128]{2,1,0:T(8,128)(2,1)S(1)} %pad_maximum_fusion), channel_id=1, source_target_pairs={{0,12},{1,13},{2,14},{3,15},{4,8},{5,9},{6,10},{7,11},{8,4},{9,5},... | collective-permute-start | bytes 196616 | tf_op jit(solution)/shard_map/ppermute | solution.py:264
  10.7 4.3 %collective-permute-start.1 = (bf16[2,128,128]{2,1,0:T(8,128)(2,1)S(1)}, bf16[2,128,128]{2,1,0:T(8,128)(2,1)S(1)}, u32[]{:S(2)}, u32[]{:S(2)}) collective-permute-start(bf16[2,128,128]{2,1,0:T(8,128)(2,1)S(1)} %pad_maximum_fusion), channel_id=1, source_target_pairs={{0,4},{1,5},{2,6},{3,7},{4,0},{5,1},{6,2},{7,3},{8,12},{9,13},{10,... | collective-permute-start | bytes 196616 | tf_op jit(solution)/shard_map/ppermute | solution.py:264
  10.7 6.0 %slice-start = ((s8[8388608]{0:T(1024)(128)(4,1)}), s8[4194304]{0:T(1024)(128)(4,1)S(1)}, s32[]{:S(2)}) async-start(s8[8388608]{0:T(1024)(128)(4,1)} %bitcast.12), calls=%async_computation | async-start | bytes 8388608
  10.7 6.0 %slice-start.1 = ((s8[8388608]{0:T(1024)(128)(4,1)}), s8[4194304]{0:T(1024)(128)(4,1)S(1)}, s32[]{:S(2)}) async-start(s8[8388608]{0:T(1024)(128)(4,1)} %bitcast.12), calls=%async_computation.1 | async-start | bytes 8388608
  15.0 1.6 %collective-permute-start.4 = (bf16[8,128,128]{2,1,0:T(8,128)(2,1)S(1)}, bf16[8,128,128]{2,1,0:T(8,128)(2,1)S(1)}, u32[]{:S(2)}, u32[]{:S(2)}) collective-permute-start(bf16[8,128,128]{2,1,0:T(8,128)(2,1)S(1)} %constant_dynamic-update-slice_fusion.mine_ref), channel_id=1, source_target_pairs={{0,1},{1,0},{2,3},{3,2},{4,5},{5,4},{6,7},{7,6},{8,9},{9,8},{10,11... | collective-permute-start | bytes 786440 | tf_op jit(solution)/shard_map/ppermute | solution.py:286
  20.3 9.4 %collective-permute-start.5 = (bf16[64,1024]{1,0:T(8,128)(2,1)S(1)}, bf16[64,1024]{1,0:T(8,128)(2,1)S(1)}, u32[]{:S(2)}, u32[]{:S(2)}) collective-permute-start(bf16[64,1024]{1,0:T(8,128)(2,1)S(1)} %get-tuple-element.26), channel_id=1, source_target_pairs={{0,128},{16,144},{32,160},{48,176},{64,192},{80,208},{96,224},{112... | collective-permute-start | bytes 393224 | tf_op jit(solution)/shard_map/ppermute | solution.py:290
  22.7 7.0 %collective-permute-start.10 = (bf16[32,1024]{1,0:T(8,128)(2,1)S(1)}, bf16[32,1024]{1,0:T(8,128)(2,1)S(1)}, u32[]{:S(2)}, u32[]{:S(2)}) collective-permute-start(bf16[32,1024]{1,0:T(8,128)(2,1)S(1)} %get-tuple-element.31), channel_id=1, source_target_pairs={{0,64},{16,80},{32,96},{48,112},{64,0},{80,16},{96,32},{112,48},{1... | collective-permute-start | bytes 196616 | tf_op jit(solution)/shard_map/ppermute | solution.py:290
  24.0 5.6 %collective-permute-start.11 = (bf16[32,1024]{1,0:T(8,128)(2,1)S(1)}, bf16[32,1024]{1,0:T(8,128)(2,1)S(1)}, u32[]{:S(2)}, u32[]{:S(2)}) collective-permute-start(bf16[32,1024]{1,0:T(8,128)(2,1)S(1)} %get-tuple-element.32), channel_id=1, source_target_pairs={{0,192},{16,208},{32,224},{48,240},{64,128},{80,144},{96,160},{112... | collective-permute-start | bytes 196616 | tf_op jit(solution)/shard_map/ppermute | solution.py:290
  24.5 12.5 %collective-permute-start.6 = (bf16[32,1024]{1,0:T(8,128)(2,1)S(1)}, bf16[32,1024]{1,0:T(8,128)(2,1)S(1)}, u32[]{:S(2)}, u32[]{:S(2)}) collective-permute-start(bf16[32,1024]{1,0:T(8,128)(2,1)S(1)} %get-tuple-element.27), channel_id=1, source_target_pairs={{0,64},{16,80},{32,96},{48,112},{64,0},{80,16},{96,32},{112,48},{1... | collective-permute-start | bytes 196616 | tf_op jit(solution)/shard_map/ppermute | solution.py:290
  25.1 11.8 %collective-permute-start.7 = (bf16[32,1024]{1,0:T(8,128)(2,1)S(1)}, bf16[32,1024]{1,0:T(8,128)(2,1)S(1)}, u32[]{:S(2)}, u32[]{:S(2)}) collective-permute-start(bf16[32,1024]{1,0:T(8,128)(2,1)S(1)} %get-tuple-element.28), channel_id=1, source_target_pairs={{0,192},{16,208},{32,224},{48,240},{64,128},{80,144},{96,160},{112... | collective-permute-start | bytes 196616 | tf_op jit(solution)/shard_map/ppermute | solution.py:290
  29.7 9.2 %collective-permute-start.12 = (bf16[16,1024]{1,0:T(8,128)(2,1)S(1)}, bf16[16,1024]{1,0:T(8,128)(2,1)S(1)}, u32[]{:S(2)}, u32[]{:S(2)}) collective-permute-start(bf16[16,1024]{1,0:T(8,128)(2,1)S(1)} %get-tuple-element.34), channel_id=1, source_target_pairs={{0,32},{16,48},{32,0},{48,16},{64,96},{80,112},{96,64},{112,80},{1... | collective-permute-start | bytes 98312 | tf_op jit(solution)/shard_map/ppermute | solution.py:291
  37.0 6.1 %collective-permute-start.8 = (bf16[16,1024]{1,0:T(8,128)(2,1)S(1)}, bf16[16,1024]{1,0:T(8,128)(2,1)S(1)}, u32[]{:S(2)}, u32[]{:S(2)}) collective-permute-start(bf16[16,1024]{1,0:T(8,128)(2,1)S(1)} %get-tuple-element.29), channel_id=1, source_target_pairs={{0,48},{16,32},{32,16},{48,0},{64,112},{80,96},{96,80},{112,64},{1... | collective-permute-start | bytes 98312 | tf_op jit(solution)/shard_map/ppermute | solution.py:291
  37.1 6.0 %collective-permute-start.9 = (bf16[16,1024]{1,0:T(8,128)(2,1)S(1)}, bf16[16,1024]{1,0:T(8,128)(2,1)S(1)}, u32[]{:S(2)}, u32[]{:S(2)}) collective-permute-start(bf16[16,1024]{1,0:T(8,128)(2,1)S(1)} %get-tuple-element.30), channel_id=1, source_target_pairs={{0,16},{16,0},{32,48},{48,32},{64,80},{80,64},{96,112},{112,96},{1... | collective-permute-start | bytes 98312 | tf_op jit(solution)/shard_map/ppermute | solution.py:291

commit v4 on v3

--- a/solution.py
+++ b/solution.py
@@ -21,6 +21,7 @@
 SIDE = 4
 ORDER = (2, 1, 3)
 STEPS = (0, 1, 3, 2)
+PARTED = ((3, 1), (0, 2))
 
 
 def factors_kernel(act_hbm, cot_hbm, down_hbm, proj_hbm, out_ref, act, cot, down, proj, both, sems):
@@ -92,6 +93,10 @@
     return lax.dot_general(left, right, NT, preferred_element_type=F32).astype(BF16)
 
 
+def place(zhi):
+    return zhi % 2 * 2 + zhi // 2
+
+
 def shard_of(k, flip):
     corpus = lax.axis_index("corpus")
     x, zlo, core = corpus // 4, (corpus // 2) % 2, corpus % 2
@@ -101,7 +106,7 @@
 def row_of(shard, rows):
     ckpt = lax.axis_index("ckpt")
     y, zhi = ckpt // SIDE, ckpt % SIDE
-    at = ((shard // SIDE) ^ y) * SIDE + ((shard % SIDE) ^ zhi)
+    at = ((shard // SIDE) ^ y) * SIDE + (place(shard % SIDE) + SIDE - place(zhi)) % SIDE
     return pl.multiple_of(at * rows, rows)
 
 
@@ -198,7 +203,7 @@
     for k, pair in ((0, (home, home)), (2, (cross, cross)), (1, (a1, b1)), (3, (a3, b3))):
         for first, out in enumerate(pair):
             for half in range(2):
-                row = (k * SIDE + first + 2 * half) * rows
+                row = (k * SIDE + PARTED[first][half]) * rows
                 at = out.shape[0] - (4 - 2 * first) * rows if out.shape[0] > 2 * rows else 0
                 at += half * rows
                 out[at : at + rows] = moved[row : row + rows]
@@ -288,11 +293,15 @@
     near_part = near_grads(ids, mine, store.shape[1])
     home, cross, a1, a3, b1, b3 = scores(ids, near_part, other, chosen, weight, store)
     over_y = lambda x, k: lax.ppermute(x, "ckpt", [(i, i ^ (4 * k)) for i in range(16)])
-    over_z = lambda x, k: lax.ppermute(x, "ckpt", [(i, i ^ k) for i in range(16)])
+
+    def over_z(x, step):
+        pairs = [(i, i // 4 * 4 + place((place(i % 4) + step) % 4)) for i in range(16)]
+        return lax.ppermute(x, "ckpt", pairs)
+
     cross = over_y(cross, 2)
-    mine, two = add(0, home, cross, over_y(a1, 1), over_y(a3, 3))
-    one, three = add(2 * ROWS, home, cross, over_y(b1, 1), over_y(b3, 3))
-    return total(over_z(three, 3), over_z(one, 1), mine, over_z(two, 2))
+    three, one = add(0, home, cross, over_y(a1, 1), over_y(a3, 3))
+    mine, two = add(2 * ROWS, home, cross, over_y(b1, 1), over_y(b3, 3))
+    return total(mine, over_z(two, 2), over_z(three, 3), over_z(one, 1))
 
 
 def solution(mesh):

time: 43.9 us -> 43.5 us (level)
  waiting for transfers between devices: 12 us -> 11.1 us
  starting transfers between devices: 22.3 us -> 22.8 us
    ppermute x3, waiting for transfers between devices: 4.44 us -> 3.59 us  [over_z(): return lax.ppermute(x, 'ckpt', pairs)]
where the time goes in v4:
time: 43.5 us; the launch traced here: 43.4 us
  starting transfers between devices  22.8 us (52%)
  waiting for transfers between devices  11.1 us (26%)
  Pallas kernels  8.65 us (20%)
  between operations  0.74 us (2%)
    ppermute x3, starting transfers between devices, over_z(): return lax.ppermute(x, 'ckpt', pairs)  9.37 us
    ppermute x5, starting transfers between devices, shards(): lax.ppermute(x, 'ckpt', [(i, i ^ 4 * k) for i in range(16)])  7.04 us
    ppermute x3, starting transfers between devices, along(): lax.ppermute(parts[k], axis, [(i, shift(i, k)) for i in range(n)])  4.26 us
    pallas_call x1, Pallas kernels, scores(): pl.pallas_call(scores_kernel, out_shape=[jax.ShapeDtypeStruct((4 * ROWS,...  3.62 us
    ppermute x3, waiting for transfers between devices, over_z(): return lax.ppermute(x, 'ckpt', pairs)  3.59 us
    ppermute x3, waiting for transfers between devices, along(): lax.ppermute(parts[k], axis, [(i, shift(i, k)) for i in range(n)])  3.08 us
    pallas_call x1, Pallas kernels, factors(): pl.pallas_call(factors_kernel, out_shape=jax.ShapeDtypeStruct((rank + wid...  2.39 us
    ppermute x5, waiting for transfers between devices, shards(): lax.ppermute(x, 'ckpt', [(i, i ^ 4 * k) for i in range(16)])  2.32 us
  transfers between devices with their start and end apart: 13, of which 7 were waited for; matrix products, arithmetic and copies ran while one was open for 0% of the time, Pallas kernels for 5%

profile of v4, /device:TPU:8, one launch (start us, length us, event | category | flops | bytes accessed | tf_op | source)
XLA Modules:
  0.0 43.4 jit_solution(15811135693281983756)
XLA Ops:
  0.0 2.4 %factors.1 = bf16[128,128]{1,0:T(8,128)(2,1)S(1)} custom-call(bf16[128,4096]{1,0:T(8,128)(2,1)} %bitcast.17, bf16[128,4096]{1,0:T(8,128)(2,1)} %bitcast.18, bf16[64,4096]{1,0:T(8,128)(2,1)} %bitcast.19, bf16[64,4096]{1,0:T(8,128)(2,1)} %bitcast.20), custom_call_target="tpu_custom_call" | custom-call | tf_op jit(solution)/shard_map/factors/pallas_call | solution.py:60
  2.4 2.0 %collective-permute-start = (bf16[128,128]{1,0:T(8,128)(2,1)S(1)}, bf16[128,128]{1,0:T(8,128)(2,1)S(1)}, u32[]{:S(2)}, u32[]{:S(2)}) collective-permute-start(bf16[128,128]{1,0:T(8,128)(2,1)S(1)} %factors.1), channel_id=1, source_target_pairs={{0,2},{1,3},{2,0},{3,1},{4,6},{5,7},{6,4},{7,5},{8,10},{9,11},{10,... | collective-permute-start | bytes 98312 | tf_op jit(solution)/shard_map/ppermute | solution.py:284
  5.1 1.3 %collective-permute-done.after_hbm = bf16[128,128]{1,0:T(8,128)(2,1)S(1)} collective-permute-done((bf16[128,128]{1,0:T(8,128)(2,1)S(1)}, bf16[128,128]{1,0:T(8,128)(2,1)S(1)}, u32[]{:S(2)}, u32[]{:S(2)}) %collective-permute-start) | collective-permute-done | bytes 32800 | tf_op jit(solution)/shard_map/ppermute | solution.py:284
  6.4 3.1 %collective-permute-start.3 = (bf16[2,128,128]{2,1,0:T(8,128)(2,1)S(1)}, bf16[2,128,128]{2,1,0:T(8,128)(2,1)S(1)}, u32[]{:S(2)}, u32[]{:S(2)}) collective-permute-start(bf16[2,128,128]{2,1,0:T(8,128)(2,1)S(1)} %pad_maximum_fusion), channel_id=1, source_target_pairs={{0,8},{1,9},{2,10},{3,11},{4,12},{5,13},{6,14},{7,15},{8,0},{9,1},... | collective-permute-start | bytes 196616 | tf_op jit(solution)/shard_map/ppermute | solution.py:269
  9.5 1.1 %collective-permute-start.2 = (bf16[2,128,128]{2,1,0:T(8,128)(2,1)S(1)}, bf16[2,128,128]{2,1,0:T(8,128)(2,1)S(1)}, u32[]{:S(2)}, u32[]{:S(2)}) collective-permute-start(bf16[2,128,128]{2,1,0:T(8,128)(2,1)S(1)} %pad_maximum_fusion), channel_id=1, source_target_pairs={{0,12},{1,13},{2,14},{3,15},{4,8},{5,9},{6,10},{7,11},{8,4},{9,5},... | collective-permute-start | bytes 196616 | tf_op jit(solution)/shard_map/ppermute | solution.py:269
  10.7 1.2 %choose.1 = (bf16[1024,1024]{1,0:T(8,128)(2,1)S(1)}, f32[8,128]{1,0:T(8,128)S(1)}, s32[16,128]{1,0:T(8,128)S(1)}) custom-call(s32[1]{0:T(128)S(6)} %copy.13.rate_ref, s32[1,1024]{1,0:T(1,128)} %bitcast.21, s32[16,128]{1,0:T(8,128)} %ids_hbm.1, bf16[128,128]{1,0:T(8,128)(2,1)S(1)} %collective-permute-done.after_hbm), custom_call_target="tpu_custom_call" | custom-call | flops 10000000000 | bytes 2097152 | tf_op jit(solution)/shard_map/choose/pallas_call | solution.py:135
  11.9 3.0 %collective-permute-done.1 = bf16[2,128,128]{2,1,0:T(8,128)(2,1)S(1)} collective-permute-done((bf16[2,128,128]{2,1,0:T(8,128)(2,1)S(1)}, bf16[2,128,128]{2,1,0:T(8,128)(2,1)S(1)}, u32[]{:S(2)}, u32[]{:S(2)}) %collective-permute-start.1) | collective-permute-done | bytes 65568 | tf_op jit(solution)/shard_map/ppermute | solution.py:269
  14.9 0.1 collective-permute-done.2
  15.0 0.1 collective-permute-start.4
  15.1 0.7 %near_grads.1.near_ref = bf16[128,4096]{1,0:T(8,128)(2,1)S(1)} custom-call(s32[16,128]{1,0:T(8,128)S(1)} %get-tuple-element.20.ids_ref, bf16[8,128,128]{2,1,0:T(8,128)(2,1)S(1)} %constant_dynamic-update-slice_fusion.mine_ref), custom_call_target="tpu_custom_call" | custom-call | flops 1000000000 | bytes 2097152 | tf_op jit(solution)/shard_map/near_grads/pallas_call | solution.py:164
  15.9 0.8 %collective-permute-done.4.other_ref = bf16[8,128,128]{2,1,0:T(8,128)(2,1)S(1)} collective-permute-done((bf16[8,128,128]{2,1,0:T(8,128)(2,1)S(1)}, bf16[8,128,128]{2,1,0:T(8,128)(2,1)S(1)}, u32[]{:S(2)}, u32[]{:S(2)}) %collective-permute-start.4) | collective-permute-done | bytes 262176 | tf_op jit(solution)/shard_map/ppermute | solution.py:291
  16.7 3.6 %scores.1 = (bf16[64,1024]{1,0:T(8,128)(2,1)S(1)}, bf16[64,1024]{1,0:T(8,128)(2,1)S(1)}, bf16[32,1024]{1,0:T(8,128)(2,1)S(1)}, bf16[32,1024]{1,0:T(8,128)(2,1)S(...) custom-call(s32[16,128]{1,0:T(8,128)S(1)} %get-tuple-element.20.ids_ref, ...), custom_call_target="tpu_custom_call" | custom-call | tf_op jit(solution)/shard_map/scores/pallas_call | solution.py:214
  20.3 2.4 %collective-permute-start.5 = (bf16[64,1024]{1,0:T(8,128)(2,1)S(1)}, bf16[64,1024]{1,0:T(8,128)(2,1)S(1)}, u32[]{:S(2)}, u32[]{:S(2)}) collective-permute-start(bf16[64,1024]{1,0:T(8,128)(2,1)S(1)} %get-tuple-element.26), channel_id=1, source_target_pairs={{0,128},{16,144},{32,160},{48,176},{64,192},{80,208},{96,224},{112... | collective-permute-start | bytes 393224 | tf_op jit(solution)/shard_map/ppermute | solution.py:295
  22.7 1.3 %collective-permute-start.9 = (bf16[32,1024]{1,0:T(8,128)(2,1)S(1)}, bf16[32,1024]{1,0:T(8,128)(2,1)S(1)}, u32[]{:S(2)}, u32[]{:S(2)}) collective-permute-start(bf16[32,1024]{1,0:T(8,128)(2,1)S(1)} %get-tuple-element.31), channel_id=1, source_target_pairs={{0,64},{16,80},{32,96},{48,112},{64,0},{80,16},{96,32},{112,48},{1... | collective-permute-start | bytes 196616 | tf_op jit(solution)/shard_map/ppermute | solution.py:295
  24.0 0.4 %collective-permute-start.10 = (bf16[32,1024]{1,0:T(8,128)(2,1)S(1)}, bf16[32,1024]{1,0:T(8,128)(2,1)S(1)}, u32[]{:S(2)}, u32[]{:S(2)}) collective-permute-start(bf16[32,1024]{1,0:T(8,128)(2,1)S(1)} %get-tuple-element.32), channel_id=1, source_target_pairs={{0,192},{16,208},{32,224},{48,240},{64,128},{80,144},{96,160},{112... | collective-permute-start | bytes 196616 | tf_op jit(solution)/shard_map/ppermute | solution.py:295
  24.5 0.7 %collective-permute-start.6 = (bf16[32,1024]{1,0:T(8,128)(2,1)S(1)}, bf16[32,1024]{1,0:T(8,128)(2,1)S(1)}, u32[]{:S(2)}, u32[]{:S(2)}) collective-permute-start(bf16[32,1024]{1,0:T(8,128)(2,1)S(1)} %get-tuple-element.27), channel_id=1, source_target_pairs={{0,64},{16,80},{32,96},{48,112},{64,0},{80,16},{96,32},{112,48},{1... | collective-permute-start | bytes 196616 | tf_op jit(solution)/shard_map/ppermute | solution.py:295
  25.1 2.2 %collective-permute-start.7 = (bf16[32,1024]{1,0:T(8,128)(2,1)S(1)}, bf16[32,1024]{1,0:T(8,128)(2,1)S(1)}, u32[]{:S(2)}, u32[]{:S(2)}) collective-permute-start(bf16[32,1024]{1,0:T(8,128)(2,1)S(1)} %get-tuple-element.28), channel_id=1, source_target_pairs={{0,192},{16,208},{32,224},{48,240},{64,128},{80,144},{96,160},{112... | collective-permute-start | bytes 196616 | tf_op jit(solution)/shard_map/ppermute | solution.py:295
  27.3 2.3 %collective-permute-done.9.refs_2_ = bf16[32,1024]{1,0:T(8,128)(2,1)S(1)} collective-permute-done((bf16[32,1024]{1,0:T(8,128)(2,1)S(1)}, bf16[32,1024]{1,0:T(8,128)(2,1)S(1)}, u32[]{:S(2)}, u32[]{:S(2)}) %collective-permute-start.9) | collective-permute-done | bytes 65568 | tf_op jit(solution)/shard_map/ppermute | solution.py:295
  29.7 6.4 %collective-permute-start.11 = (bf16[16,1024]{1,0:T(8,128)(2,1)S(1)}, bf16[16,1024]{1,0:T(8,128)(2,1)S(1)}, u32[]{:S(2)}, u32[]{:S(2)}) collective-permute-start(bf16[16,1024]{1,0:T(8,128)(2,1)S(1)} %get-tuple-element.33), channel_id=1, source_target_pairs={{0,48},{16,32},{32,0},{48,16},{64,112},{80,96},{96,64},{112,80},{1... | collective-permute-start | bytes 98312 | tf_op jit(solution)/shard_map/ppermute | solution.py:299
  36.1 1.0 %collective-permute-start.12 = (bf16[16,1024]{1,0:T(8,128)(2,1)S(1)}, bf16[16,1024]{1,0:T(8,128)(2,1)S(1)}, u32[]{:S(2)}, u32[]{:S(2)}) collective-permute-start(bf16[16,1024]{1,0:T(8,128)(2,1)S(1)} %get-tuple-element.34), channel_id=1, source_target_pairs={{0,32},{16,48},{32,16},{48,0},{64,96},{80,112},{96,80},{112,64},{1... | collective-permute-start | bytes 98312 | tf_op jit(solution)/shard_map/ppermute | solution.py:299
  37.1 2.0 %collective-permute-start.8 = (bf16[16,1024]{1,0:T(8,128)(2,1)S(1)}, bf16[16,1024]{1,0:T(8,128)(2,1)S(1)}, u32[]{:S(2)}, u32[]{:S(2)}) collective-permute-start(bf16[16,1024]{1,0:T(8,128)(2,1)S(1)} %get-tuple-element.30), channel_id=1, source_target_pairs={{0,16},{16,0},{32,48},{48,32},{64,80},{80,64},{96,112},{112,96},{1... | collective-permute-start | bytes 98312 | tf_op jit(solution)/shard_map/ppermute | solution.py:299
  39.1 3.2 %collective-permute-done.12.d = bf16[16,1024]{1,0:T(8,128)(2,1)S(1)} collective-permute-done((bf16[16,1024]{1,0:T(8,128)(2,1)S(1)}, bf16[16,1024]{1,0:T(8,128)(2,1)S(1)}, u32[]{:S(2)}, u32[]{:S(2)}) %collective-permute-start.12) | collective-permute-done | bytes 32800 | tf_op jit(solution)/shard_map/ppermute | solution.py:299
  42.3 0.4 collective-permute-done.8.b
  42.7 0.6 %total.1 = f32[16,1024]{1,0:T(8,128)} custom-call(bf16[16,1024]{1,0:T(8,128)(2,1)S(1)} %get-tuple-element.29.a, bf16[16,1024]{1,0:T(8,128)(2,1)S(1)} %collective-permute-done.8.b, bf16[16,1024]{1,0:T(8,128)(2,1)S(1)} %collective-permute-done.11.c, bf16[16,1024]{1,0:T(8,128)(2,1)S(1)} %collective-permute-done.12.d), custom_call_target="tpu_custom_call" | custom-call | tf_op jit(solution)/shard_map/total/pallas_call | solution.py:256
  (20 shorter events, 0.2 us)
Async XLA Ops:
  2.4 4.0 %collective-permute-start = (bf16[128,128]{1,0:T(8,128)(2,1)S(1)}, bf16[128,128]{1,0:T(8,128)(2,1)S(1)}, u32[]{:S(2)}, u32[]{:S(2)}) collective-permute-start(bf16[128,128]{1,0:T(8,128)(2,1)S(1)} %factors.1), channel_id=1, source_target_pairs={{0,2},{1,3},{2,0},{3,1},{4,6},{5,7},{6,4},{7,5},{8,10},{9,11},{10,... | collective-permute-start | bytes 98312 | tf_op jit(solution)/shard_map/ppermute | solution.py:284
  6.4 8.6 %collective-permute-start.3 = (bf16[2,128,128]{2,1,0:T(8,128)(2,1)S(1)}, bf16[2,128,128]{2,1,0:T(8,128)(2,1)S(1)}, u32[]{:S(2)}, u32[]{:S(2)}) collective-permute-start(bf16[2,128,128]{2,1,0:T(8,128)(2,1)S(1)} %pad_maximum_fusion), channel_id=1, source_target_pairs={{0,8},{1,9},{2,10},{3,11},{4,12},{5,13},{6,14},{7,15},{8,0},{9,1},... | collective-permute-start | bytes 196616 | tf_op jit(solution)/shard_map/ppermute | solution.py:269
  9.5 5.5 %collective-permute-start.2 = (bf16[2,128,128]{2,1,0:T(8,128)(2,1)S(1)}, bf16[2,128,128]{2,1,0:T(8,128)(2,1)S(1)}, u32[]{:S(2)}, u32[]{:S(2)}) collective-permute-start(bf16[2,128,128]{2,1,0:T(8,128)(2,1)S(1)} %pad_maximum_fusion), channel_id=1, source_target_pairs={{0,12},{1,13},{2,14},{3,15},{4,8},{5,9},{6,10},{7,11},{8,4},{9,5},... | collective-permute-start | bytes 196616 | tf_op jit(solution)/shard_map/ppermute | solution.py:269
  10.7 4.3 %collective-permute-start.1 = (bf16[2,128,128]{2,1,0:T(8,128)(2,1)S(1)}, bf16[2,128,128]{2,1,0:T(8,128)(2,1)S(1)}, u32[]{:S(2)}, u32[]{:S(2)}) collective-permute-start(bf16[2,128,128]{2,1,0:T(8,128)(2,1)S(1)} %pad_maximum_fusion), channel_id=1, source_target_pairs={{0,4},{1,5},{2,6},{3,7},{4,0},{5,1},{6,2},{7,3},{8,12},{9,13},{10,... | collective-permute-start | bytes 196616 | tf_op jit(solution)/shard_map/ppermute | solution.py:269
  10.7 6.0 %slice-start = ((s8[8388608]{0:T(1024)(128)(4,1)}), s8[4194304]{0:T(1024)(128)(4,1)S(1)}, s32[]{:S(2)}) async-start(s8[8388608]{0:T(1024)(128)(4,1)} %bitcast.12), calls=%async_computation | async-start | bytes 8388608
  10.7 6.0 %slice-start.1 = ((s8[8388608]{0:T(1024)(128)(4,1)}), s8[4194304]{0:T(1024)(128)(4,1)S(1)}, s32[]{:S(2)}) async-start(s8[8388608]{0:T(1024)(128)(4,1)} %bitcast.12), calls=%async_computation.1 | async-start | bytes 8388608
  15.0 1.6 %collective-permute-start.4 = (bf16[8,128,128]{2,1,0:T(8,128)(2,1)S(1)}, bf16[8,128,128]{2,1,0:T(8,128)(2,1)S(1)}, u32[]{:S(2)}, u32[]{:S(2)}) collective-permute-start(bf16[8,128,128]{2,1,0:T(8,128)(2,1)S(1)} %constant_dynamic-update-slice_fusion.mine_ref), channel_id=1, source_target_pairs={{0,1},{1,0},{2,3},{3,2},{4,5},{5,4},{6,7},{7,6},{8,9},{9,8},{10,11... | collective-permute-start | bytes 786440 | tf_op jit(solution)/shard_map/ppermute | solution.py:291
  20.3 9.4 %collective-permute-start.5 = (bf16[64,1024]{1,0:T(8,128)(2,1)S(1)}, bf16[64,1024]{1,0:T(8,128)(2,1)S(1)}, u32[]{:S(2)}, u32[]{:S(2)}) collective-permute-start(bf16[64,1024]{1,0:T(8,128)(2,1)S(1)} %get-tuple-element.26), channel_id=1, source_target_pairs={{0,128},{16,144},{32,160},{48,176},{64,192},{80,208},{96,224},{112... | collective-permute-start | bytes 393224 | tf_op jit(solution)/shard_map/ppermute | solution.py:295
  22.7 7.0 %collective-permute-start.9 = (bf16[32,1024]{1,0:T(8,128)(2,1)S(1)}, bf16[32,1024]{1,0:T(8,128)(2,1)S(1)}, u32[]{:S(2)}, u32[]{:S(2)}) collective-permute-start(bf16[32,1024]{1,0:T(8,128)(2,1)S(1)} %get-tuple-element.31), channel_id=1, source_target_pairs={{0,64},{16,80},{32,96},{48,112},{64,0},{80,16},{96,32},{112,48},{1... | collective-permute-start | bytes 196616 | tf_op jit(solution)/shard_map/ppermute | solution.py:295
  24.0 5.6 %collective-permute-start.10 = (bf16[32,1024]{1,0:T(8,128)(2,1)S(1)}, bf16[32,1024]{1,0:T(8,128)(2,1)S(1)}, u32[]{:S(2)}, u32[]{:S(2)}) collective-permute-start(bf16[32,1024]{1,0:T(8,128)(2,1)S(1)} %get-tuple-element.32), channel_id=1, source_target_pairs={{0,192},{16,208},{32,224},{48,240},{64,128},{80,144},{96,160},{112... | collective-permute-start | bytes 196616 | tf_op jit(solution)/shard_map/ppermute | solution.py:295
  24.5 12.6 %collective-permute-start.6 = (bf16[32,1024]{1,0:T(8,128)(2,1)S(1)}, bf16[32,1024]{1,0:T(8,128)(2,1)S(1)}, u32[]{:S(2)}, u32[]{:S(2)}) collective-permute-start(bf16[32,1024]{1,0:T(8,128)(2,1)S(1)} %get-tuple-element.27), channel_id=1, source_target_pairs={{0,64},{16,80},{32,96},{48,112},{64,0},{80,16},{96,32},{112,48},{1... | collective-permute-start | bytes 196616 | tf_op jit(solution)/shard_map/ppermute | solution.py:295
  25.1 11.9 %collective-permute-start.7 = (bf16[32,1024]{1,0:T(8,128)(2,1)S(1)}, bf16[32,1024]{1,0:T(8,128)(2,1)S(1)}, u32[]{:S(2)}, u32[]{:S(2)}) collective-permute-start(bf16[32,1024]{1,0:T(8,128)(2,1)S(1)} %get-tuple-element.28), channel_id=1, source_target_pairs={{0,192},{16,208},{32,224},{48,240},{64,128},{80,144},{96,160},{112... | collective-permute-start | bytes 196616 | tf_op jit(solution)/shard_map/ppermute | solution.py:295
  29.7 9.4 %collective-permute-start.11 = (bf16[16,1024]{1,0:T(8,128)(2,1)S(1)}, bf16[16,1024]{1,0:T(8,128)(2,1)S(1)}, u32[]{:S(2)}, u32[]{:S(2)}) collective-permute-start(bf16[16,1024]{1,0:T(8,128)(2,1)S(1)} %get-tuple-element.33), channel_id=1, source_target_pairs={{0,48},{16,32},{32,0},{48,16},{64,112},{80,96},{96,64},{112,80},{1... | collective-permute-start | bytes 98312 | tf_op jit(solution)/shard_map/ppermute | solution.py:299
  36.1 6.2 %collective-permute-start.12 = (bf16[16,1024]{1,0:T(8,128)(2,1)S(1)}, bf16[16,1024]{1,0:T(8,128)(2,1)S(1)}, u32[]{:S(2)}, u32[]{:S(2)}) collective-permute-start(bf16[16,1024]{1,0:T(8,128)(2,1)S(1)} %get-tuple-element.34), channel_id=1, source_target_pairs={{0,32},{16,48},{32,16},{48,0},{64,96},{80,112},{96,80},{112,64},{1... | collective-permute-start | bytes 98312 | tf_op jit(solution)/shard_map/ppermute | solution.py:299
  37.1 5.6 %collective-permute-start.8 = (bf16[16,1024]{1,0:T(8,128)(2,1)S(1)}, bf16[16,1024]{1,0:T(8,128)(2,1)S(1)}, u32[]{:S(2)}, u32[]{:S(2)}) collective-permute-start(bf16[16,1024]{1,0:T(8,128)(2,1)S(1)} %get-tuple-element.30), channel_id=1, source_target_pairs={{0,16},{16,0},{32,48},{48,32},{64,80},{80,64},{96,112},{112,96},{1... | collective-permute-start | bytes 98312 | tf_op jit(solution)/shard_map/ppermute | solution.py:299

commit v5 on v4

--- a/solution.py
+++ b/solution.py
@@ -20,7 +20,7 @@
 ROWS = 16
 SIDE = 4
 ORDER = (2, 1, 3)
-STEPS = (0, 1, 3, 2)
+STEPS = (0, 1, 2, 3)
 PARTED = ((3, 1), (0, 2))
 
 
@@ -199,14 +199,13 @@
         placed[:, at] = (part * weight).astype(BF16)
 
     moved = lax.dot_general(placed[...], choose_ref[...], NT, preferred_element_type=F32)
-    moved = moved.astype(BF16)
-    for k, pair in ((0, (home, home)), (2, (cross, cross)), (1, (a1, b1)), (3, (a3, b3))):
+    for k, pair in ((0, (home, home)), (3, (cross, cross)), (2, (a1, b1)), (1, (a3, b3))):
         for first, out in enumerate(pair):
             for half in range(2):
                 row = (k * SIDE + PARTED[first][half]) * rows
                 at = out.shape[0] - (4 - 2 * first) * rows if out.shape[0] > 2 * rows else 0
                 at += half * rows
-                out[at : at + rows] = moved[row : row + rows]
+                out[at : at + rows] = moved[row : row + rows].astype(out.dtype)
 
 
 def scores(ids, near, other, chosen, weight, store):
@@ -240,7 +239,8 @@
     columns = parts[0].shape[1]
     return pl.pallas_call(
         functools.partial(add_kernel, first),
-        out_shape=[jax.ShapeDtypeStruct((ROWS, columns), BF16)] * 2,
+        out_shape=[jax.ShapeDtypeStruct((ROWS, columns), F32 if first else BF16)]
+        + [jax.ShapeDtypeStruct((ROWS, columns), BF16)],
         in_specs=[VMEM] * SIDE,
         out_specs=[VMEM] * 2,
         compiler_params=pltpu.CompilerParams(vmem_limit_bytes=4 * MIB),
@@ -298,9 +298,9 @@
         pairs = [(i, i // 4 * 4 + place((place(i % 4) + step) % 4)) for i in range(16)]
         return lax.ppermute(x, "ckpt", pairs)
 
-    cross = over_y(cross, 2)
-    three, one = add(0, home, cross, over_y(a1, 1), over_y(a3, 3))
-    mine, two = add(2 * ROWS, home, cross, over_y(b1, 1), over_y(b3, 3))
+    cross = over_y(cross, 3)
+    three, one = add(0, home, cross, over_y(a1, 2), over_y(a3, 1))
+    mine, two = add(2 * ROWS, home, cross, over_y(b1, 2), over_y(b3, 1))
     return total(mine, over_z(two, 2), over_z(three, 3), over_z(one, 1))
 
 

time: 43.5 us -> 43.1 us (level)
  the two profiles are of different devices: /device:TPU:8 before, /device:TPU:24 now
where the time goes in v5:
time: 43.1 us; the launch traced here: 43 us
  starting transfers between devices  21.2 us (49%)
  waiting for transfers between devices  12.4 us (29%)
  Pallas kernels  8.66 us (20%)
  between operations  0.73 us (2%)
    ppermute x3, starting transfers between devices, over_z(): return lax.ppermute(x, 'ckpt', pairs)  9.35 us
    ppermute x5, starting transfers between devices, shards(): lax.ppermute(x, 'ckpt', [(i, i ^ 4 * k) for i in range(16)])  5.52 us
    ppermute x3, starting transfers between devices, along(): lax.ppermute(parts[k], axis, [(i, shift(i, k)) for i in range(n)])  4.18 us
    pallas_call x1, Pallas kernels, scores(): pl.pallas_call(scores_kernel, out_shape=[jax.ShapeDtypeStruct((4 * ROWS,...  3.63 us
    ppermute x3, waiting for transfers between devices, over_z(): return lax.ppermute(x, 'ckpt', pairs)  3.6 us
    ppermute x5, waiting for transfers between devices, shards(): lax.ppermute(x, 'ckpt', [(i, i ^ 4 * k) for i in range(16)])  3.42 us
    ppermute x3, waiting for transfers between devices, along(): lax.ppermute(parts[k], axis, [(i, shift(i, k)) for i in range(n)])  3.18 us
    pallas_call x1, Pallas kernels, factors(): pl.pallas_call(factors_kernel, out_shape=jax.ShapeDtypeStruct((rank + wid...  2.39 us
  transfers between devices with their start and end apart: 13, of which 9 were waited for; matrix products, arithmetic and copies ran while one was open for 0% of the time, Pallas kernels for 5%

profile of v5, /device:TPU:24, one launch (start us, length us, event | category | flops | bytes accessed | tf_op | source)
XLA Modules:
  0.0 43.0 jit_solution(1595618387054775700)
XLA Ops:
  0.0 2.4 %factors.1 = bf16[128,128]{1,0:T(8,128)(2,1)S(1)} custom-call(bf16[128,4096]{1,0:T(8,128)(2,1)} %bitcast.17, bf16[128,4096]{1,0:T(8,128)(2,1)} %bitcast.18, bf16[64,4096]{1,0:T(8,128)(2,1)} %bitcast.19, bf16[64,4096]{1,0:T(8,128)(2,1)} %bitcast.20), custom_call_target="tpu_custom_call" | custom-call | tf_op jit(solution)/shard_map/factors/pallas_call | solution.py:60
  2.4 2.0 %collective-permute-start = (bf16[128,128]{1,0:T(8,128)(2,1)S(1)}, bf16[128,128]{1,0:T(8,128)(2,1)S(1)}, u32[]{:S(2)}, u32[]{:S(2)}) collective-permute-start(bf16[128,128]{1,0:T(8,128)(2,1)S(1)} %factors.1), channel_id=1, source_target_pairs={{0,2},{1,3},{2,0},{3,1},{4,6},{5,7},{6,4},{7,5},{8,10},{9,11},{10,... | collective-permute-start | bytes 98312 | tf_op jit(solution)/shard_map/ppermute | solution.py:284
  5.1 1.3 %collective-permute-done.after_hbm = bf16[128,128]{1,0:T(8,128)(2,1)S(1)} collective-permute-done((bf16[128,128]{1,0:T(8,128)(2,1)S(1)}, bf16[128,128]{1,0:T(8,128)(2,1)S(1)}, u32[]{:S(2)}, u32[]{:S(2)}) %collective-permute-start) | collective-permute-done | bytes 32800 | tf_op jit(solution)/shard_map/ppermute | solution.py:284
  6.4 2.8 %collective-permute-start.3 = (bf16[2,128,128]{2,1,0:T(8,128)(2,1)S(1)}, bf16[2,128,128]{2,1,0:T(8,128)(2,1)S(1)}, u32[]{:S(2)}, u32[]{:S(2)}) collective-permute-start(bf16[2,128,128]{2,1,0:T(8,128)(2,1)S(1)} %pad_maximum_fusion), channel_id=1, source_target_pairs={{0,12},{1,13},{2,14},{3,15},{4,8},{5,9},{6,10},{7,11},{8,4},{9,5},... | collective-permute-start | bytes 196616 | tf_op jit(solution)/shard_map/ppermute | solution.py:269
  9.3 0.8 %collective-permute-start.2 = (bf16[2,128,128]{2,1,0:T(8,128)(2,1)S(1)}, bf16[2,128,128]{2,1,0:T(8,128)(2,1)S(1)}, u32[]{:S(2)}, u32[]{:S(2)}) collective-permute-start(bf16[2,128,128]{2,1,0:T(8,128)(2,1)S(1)} %pad_maximum_fusion), channel_id=1, source_target_pairs={{0,8},{1,9},{2,10},{3,11},{4,12},{5,13},{6,14},{7,15},{8,0},{9,1},... | collective-permute-start | bytes 196616 | tf_op jit(solution)/shard_map/ppermute | solution.py:269
  10.1 0.5 %collective-permute-start.1 = (bf16[2,128,128]{2,1,0:T(8,128)(2,1)S(1)}, bf16[2,128,128]{2,1,0:T(8,128)(2,1)S(1)}, u32[]{:S(2)}, u32[]{:S(2)}) collective-permute-start(bf16[2,128,128]{2,1,0:T(8,128)(2,1)S(1)} %pad_maximum_fusion), channel_id=1, source_target_pairs={{0,4},{1,5},{2,6},{3,7},{4,0},{5,1},{6,2},{7,3},{8,12},{9,13},{10,... | collective-permute-start | bytes 196616 | tf_op jit(solution)/shard_map/ppermute | solution.py:269
  10.6 1.2 %choose.1 = (bf16[1024,1024]{1,0:T(8,128)(2,1)S(1)}, f32[8,128]{1,0:T(8,128)S(1)}, s32[16,128]{1,0:T(8,128)S(1)}) custom-call(s32[1]{0:T(128)S(6)} %copy.13.rate_ref, s32[1,1024]{1,0:T(1,128)} %bitcast.21, s32[16,128]{1,0:T(8,128)} %ids_hbm.1, bf16[128,128]{1,0:T(8,128)(2,1)S(1)} %collective-permute-done.after_hbm), custom_call_target="tpu_custom_call" | custom-call | flops 10000000000 | bytes 2097152 | tf_op jit(solution)/shard_map/choose/pallas_call | solution.py:135
  11.8 2.5 %collective-permute-done.1 = bf16[2,128,128]{2,1,0:T(8,128)(2,1)S(1)} collective-permute-done((bf16[2,128,128]{2,1,0:T(8,128)(2,1)S(1)}, bf16[2,128,128]{2,1,0:T(8,128)(2,1)S(1)}, u32[]{:S(2)}, u32[]{:S(2)}) %collective-permute-start.1) | collective-permute-done | bytes 65568 | tf_op jit(solution)/shard_map/ppermute | solution.py:269
  14.3 0.7 %collective-permute-done.2 = bf16[2,128,128]{2,1,0:T(8,128)(2,1)S(1)} collective-permute-done((bf16[2,128,128]{2,1,0:T(8,128)(2,1)S(1)}, bf16[2,128,128]{2,1,0:T(8,128)(2,1)S(1)}, u32[]{:S(2)}, u32[]{:S(2)}) %collective-permute-start.2) | collective-permute-done | bytes 65568 | tf_op jit(solution)/shard_map/ppermute | solution.py:269
  15.2 0.7 %near_grads.1.near_ref = bf16[128,4096]{1,0:T(8,128)(2,1)S(1)} custom-call(s32[16,128]{1,0:T(8,128)S(1)} %get-tuple-element.20.ids_ref, bf16[8,128,128]{2,1,0:T(8,128)(2,1)S(1)} %constant_dynamic-update-slice_fusion.mine_ref), custom_call_target="tpu_custom_call" | custom-call | flops 1000000000 | bytes 2097152 | tf_op jit(solution)/shard_map/near_grads/pallas_call | solution.py:164
  15.9 0.8 %collective-permute-done.4.other_ref = bf16[8,128,128]{2,1,0:T(8,128)(2,1)S(1)} collective-permute-done((bf16[8,128,128]{2,1,0:T(8,128)(2,1)S(1)}, bf16[8,128,128]{2,1,0:T(8,128)(2,1)S(1)}, u32[]{:S(2)}, u32[]{:S(2)}) %collective-permute-start.4) | collective-permute-done | bytes 262176 | tf_op jit(solution)/shard_map/ppermute | solution.py:291
  16.7 3.6 %scores.1 = (bf16[64,1024]{1,0:T(8,128)(2,1)S(1)}, bf16[64,1024]{1,0:T(8,128)(2,1)S(1)}, bf16[32,1024]{1,0:T(8,128)(2,1)S(1)}, bf16[32,1024]{1,0:T(8,128)(2,1)S(...) custom-call(s32[16,128]{1,0:T(8,128)S(1)} %get-tuple-element.20.ids_ref, ...), custom_call_target="tpu_custom_call" | custom-call | tf_op jit(solution)/shard_map/scores/pallas_call | solution.py:213
  20.3 0.6 %collective-permute-start.5 = (bf16[64,1024]{1,0:T(8,128)(2,1)S(1)}, bf16[64,1024]{1,0:T(8,128)(2,1)S(1)}, u32[]{:S(2)}, u32[]{:S(2)}) collective-permute-start(bf16[64,1024]{1,0:T(8,128)(2,1)S(1)} %get-tuple-element.26), channel_id=1, source_target_pairs={{0,192},{16,208},{32,224},{48,240},{64,128},{80,144},{96,160},{112... | collective-permute-start | bytes 393224 | tf_op jit(solution)/shard_map/ppermute | solution.py:295
  20.9 2.3 %collective-permute-start.9 = (bf16[32,1024]{1,0:T(8,128)(2,1)S(1)}, bf16[32,1024]{1,0:T(8,128)(2,1)S(1)}, u32[]{:S(2)}, u32[]{:S(2)}) collective-permute-start(bf16[32,1024]{1,0:T(8,128)(2,1)S(1)} %get-tuple-element.31), channel_id=1, source_target_pairs={{0,128},{16,144},{32,160},{48,176},{64,192},{80,208},{96,224},{112... | collective-permute-start | bytes 196616 | tf_op jit(solution)/shard_map/ppermute | solution.py:295
  23.2 1.3 %collective-permute-start.10 = (bf16[32,1024]{1,0:T(8,128)(2,1)S(1)}, bf16[32,1024]{1,0:T(8,128)(2,1)S(1)}, u32[]{:S(2)}, u32[]{:S(2)}) collective-permute-start(bf16[32,1024]{1,0:T(8,128)(2,1)S(1)} %get-tuple-element.32), channel_id=1, source_target_pairs={{0,64},{16,80},{32,96},{48,112},{64,0},{80,16},{96,32},{112,48},{1... | collective-permute-start | bytes 196616 | tf_op jit(solution)/shard_map/ppermute | solution.py:295
  24.5 1.2 %collective-permute-start.6 = (bf16[32,1024]{1,0:T(8,128)(2,1)S(1)}, bf16[32,1024]{1,0:T(8,128)(2,1)S(1)}, u32[]{:S(2)}, u32[]{:S(2)}) collective-permute-start(bf16[32,1024]{1,0:T(8,128)(2,1)S(1)} %get-tuple-element.27), channel_id=1, source_target_pairs={{0,128},{16,144},{32,160},{48,176},{64,192},{80,208},{96,224},{112... | collective-permute-start | bytes 196616 | tf_op jit(solution)/shard_map/ppermute | solution.py:295
  25.9 1.4 %collective-permute-done.9.refs_2_ = bf16[32,1024]{1,0:T(8,128)(2,1)S(1)} collective-permute-done((bf16[32,1024]{1,0:T(8,128)(2,1)S(1)}, bf16[32,1024]{1,0:T(8,128)(2,1)S(1)}, u32[]{:S(2)}, u32[]{:S(2)}) %collective-permute-start.9) | collective-permute-done | bytes 65568 | tf_op jit(solution)/shard_map/ppermute | solution.py:295
  27.3 1.6 %collective-permute-done.10.refs_3_ = bf16[32,1024]{1,0:T(8,128)(2,1)S(1)} collective-permute-done((bf16[32,1024]{1,0:T(8,128)(2,1)S(1)}, bf16[32,1024]{1,0:T(8,128)(2,1)S(1)}, u32[]{:S(2)}, u32[]{:S(2)}) %collective-permute-start.10) | collective-permute-done | bytes 65568 | tf_op jit(solution)/shard_map/ppermute | solution.py:295
  29.3 6.4 %collective-permute-start.11 = (bf16[16,1024]{1,0:T(8,128)(2,1)S(1)}, bf16[16,1024]{1,0:T(8,128)(2,1)S(1)}, u32[]{:S(2)}, u32[]{:S(2)}) collective-permute-start(bf16[16,1024]{1,0:T(8,128)(2,1)S(1)} %get-tuple-element.33), channel_id=1, source_target_pairs={{0,48},{16,32},{32,0},{48,16},{64,112},{80,96},{96,64},{112,80},{1... | collective-permute-start | bytes 98312 | tf_op jit(solution)/shard_map/ppermute | solution.py:299
  35.7 1.0 %collective-permute-start.12 = (bf16[16,1024]{1,0:T(8,128)(2,1)S(1)}, bf16[16,1024]{1,0:T(8,128)(2,1)S(1)}, u32[]{:S(2)}, u32[]{:S(2)}) collective-permute-start(bf16[16,1024]{1,0:T(8,128)(2,1)S(1)} %get-tuple-element.34), channel_id=1, source_target_pairs={{0,32},{16,48},{32,16},{48,0},{64,96},{80,112},{96,80},{112,64},{1... | collective-permute-start | bytes 98312 | tf_op jit(solution)/shard_map/ppermute | solution.py:299
  36.7 2.0 %collective-permute-start.8 = (bf16[16,1024]{1,0:T(8,128)(2,1)S(1)}, bf16[16,1024]{1,0:T(8,128)(2,1)S(1)}, u32[]{:S(2)}, u32[]{:S(2)}) collective-permute-start(bf16[16,1024]{1,0:T(8,128)(2,1)S(1)} %get-tuple-element.30), channel_id=1, source_target_pairs={{0,16},{16,0},{32,48},{48,32},{64,80},{80,64},{96,112},{112,96},{1... | collective-permute-start | bytes 98312 | tf_op jit(solution)/shard_map/ppermute | solution.py:299
  38.7 3.1 %collective-permute-done.12.d = bf16[16,1024]{1,0:T(8,128)(2,1)S(1)} collective-permute-done((bf16[16,1024]{1,0:T(8,128)(2,1)S(1)}, bf16[16,1024]{1,0:T(8,128)(2,1)S(1)}, u32[]{:S(2)}, u32[]{:S(2)}) %collective-permute-start.12) | collective-permute-done | bytes 32800 | tf_op jit(solution)/shard_map/ppermute | solution.py:299
  41.8 0.5 %collective-permute-done.8.b = bf16[16,1024]{1,0:T(8,128)(2,1)S(1)} collective-permute-done((bf16[16,1024]{1,0:T(8,128)(2,1)S(1)}, bf16[16,1024]{1,0:T(8,128)(2,1)S(1)}, u32[]{:S(2)}, u32[]{:S(2)}) %collective-permute-start.8) | collective-permute-done | bytes 32800 | tf_op jit(solution)/shard_map/ppermute | solution.py:299
  42.3 0.6 %total.1 = f32[16,1024]{1,0:T(8,128)} custom-call(f32[16,1024]{1,0:T(8,128)S(1)} %get-tuple-element.29.a, bf16[16,1024]{1,0:T(8,128)(2,1)S(1)} %collective-permute-done.8.b, bf16[16,1024]{1,0:T(8,128)(2,1)S(1)} %collective-permute-done.11.c, bf16[16,1024]{1,0:T(8,128)(2,1)S(1)} %collective-permute-done.12.d), custom_call_target="tpu_custom_call" | custom-call | tf_op jit(solution)/shard_map/total/pallas_call | solution.py:256
  (20 shorter events, 0.8 us)
Async XLA Ops:
  2.4 4.0 %collective-permute-start = (bf16[128,128]{1,0:T(8,128)(2,1)S(1)}, bf16[128,128]{1,0:T(8,128)(2,1)S(1)}, u32[]{:S(2)}, u32[]{:S(2)}) collective-permute-start(bf16[128,128]{1,0:T(8,128)(2,1)S(1)} %factors.1), channel_id=1, source_target_pairs={{0,2},{1,3},{2,0},{3,1},{4,6},{5,7},{6,4},{7,5},{8,10},{9,11},{10,... | collective-permute-start | bytes 98312 | tf_op jit(solution)/shard_map/ppermute | solution.py:284
  6.4 8.6 %collective-permute-start.3 = (bf16[2,128,128]{2,1,0:T(8,128)(2,1)S(1)}, bf16[2,128,128]{2,1,0:T(8,128)(2,1)S(1)}, u32[]{:S(2)}, u32[]{:S(2)}) collective-permute-start(bf16[2,128,128]{2,1,0:T(8,128)(2,1)S(1)} %pad_maximum_fusion), channel_id=1, source_target_pairs={{0,12},{1,13},{2,14},{3,15},{4,8},{5,9},{6,10},{7,11},{8,4},{9,5},... | collective-permute-start | bytes 196616 | tf_op jit(solution)/shard_map/ppermute | solution.py:269
  9.3 5.8 %collective-permute-start.2 = (bf16[2,128,128]{2,1,0:T(8,128)(2,1)S(1)}, bf16[2,128,128]{2,1,0:T(8,128)(2,1)S(1)}, u32[]{:S(2)}, u32[]{:S(2)}) collective-permute-start(bf16[2,128,128]{2,1,0:T(8,128)(2,1)S(1)} %pad_maximum_fusion), channel_id=1, source_target_pairs={{0,8},{1,9},{2,10},{3,11},{4,12},{5,13},{6,14},{7,15},{8,0},{9,1},... | collective-permute-start | bytes 196616 | tf_op jit(solution)/shard_map/ppermute | solution.py:269
  10.1 4.3 %collective-permute-start.1 = (bf16[2,128,128]{2,1,0:T(8,128)(2,1)S(1)}, bf16[2,128,128]{2,1,0:T(8,128)(2,1)S(1)}, u32[]{:S(2)}, u32[]{:S(2)}) collective-permute-start(bf16[2,128,128]{2,1,0:T(8,128)(2,1)S(1)} %pad_maximum_fusion), channel_id=1, source_target_pairs={{0,4},{1,5},{2,6},{3,7},{4,0},{5,1},{6,2},{7,3},{8,12},{9,13},{10,... | collective-permute-start | bytes 196616 | tf_op jit(solution)/shard_map/ppermute | solution.py:269
  10.6 6.1 %slice-start = ((s8[8388608]{0:T(1024)(128)(4,1)}), s8[4194304]{0:T(1024)(128)(4,1)S(1)}, s32[]{:S(2)}) async-start(s8[8388608]{0:T(1024)(128)(4,1)} %bitcast.12), calls=%async_computation | async-start | bytes 8388608
  10.6 6.1 %slice-start.1 = ((s8[8388608]{0:T(1024)(128)(4,1)}), s8[4194304]{0:T(1024)(128)(4,1)S(1)}, s32[]{:S(2)}) async-start(s8[8388608]{0:T(1024)(128)(4,1)} %bitcast.12), calls=%async_computation.1 | async-start | bytes 8388608
  15.1 1.6 %collective-permute-start.4 = (bf16[8,128,128]{2,1,0:T(8,128)(2,1)S(1)}, bf16[8,128,128]{2,1,0:T(8,128)(2,1)S(1)}, u32[]{:S(2)}, u32[]{:S(2)}) collective-permute-start(bf16[8,128,128]{2,1,0:T(8,128)(2,1)S(1)} %constant_dynamic-update-slice_fusion.mine_ref), channel_id=1, source_target_pairs={{0,1},{1,0},{2,3},{3,2},{4,5},{5,4},{6,7},{7,6},{8,9},{9,8},{10,11... | collective-permute-start | bytes 786440 | tf_op jit(solution)/shard_map/ppermute | solution.py:291
  20.3 8.9 %collective-permute-start.5 = (bf16[64,1024]{1,0:T(8,128)(2,1)S(1)}, bf16[64,1024]{1,0:T(8,128)(2,1)S(1)}, u32[]{:S(2)}, u32[]{:S(2)}) collective-permute-start(bf16[64,1024]{1,0:T(8,128)(2,1)S(1)} %get-tuple-element.26), channel_id=1, source_target_pairs={{0,192},{16,208},{32,224},{48,240},{64,128},{80,144},{96,160},{112... | collective-permute-start | bytes 393224 | tf_op jit(solution)/shard_map/ppermute | solution.py:295
  20.9 6.4 %collective-permute-start.9 = (bf16[32,1024]{1,0:T(8,128)(2,1)S(1)}, bf16[32,1024]{1,0:T(8,128)(2,1)S(1)}, u32[]{:S(2)}, u32[]{:S(2)}) collective-permute-start(bf16[32,1024]{1,0:T(8,128)(2,1)S(1)} %get-tuple-element.31), channel_id=1, source_target_pairs={{0,128},{16,144},{32,160},{48,176},{64,192},{80,208},{96,224},{112... | collective-permute-start | bytes 196616 | tf_op jit(solution)/shard_map/ppermute | solution.py:295
  23.2 5.6 %collective-permute-start.10 = (bf16[32,1024]{1,0:T(8,128)(2,1)S(1)}, bf16[32,1024]{1,0:T(8,128)(2,1)S(1)}, u32[]{:S(2)}, u32[]{:S(2)}) collective-permute-start(bf16[32,1024]{1,0:T(8,128)(2,1)S(1)} %get-tuple-element.32), channel_id=1, source_target_pairs={{0,64},{16,80},{32,96},{48,112},{64,0},{80,16},{96,32},{112,48},{1... | collective-permute-start | bytes 196616 | tf_op jit(solution)/shard_map/ppermute | solution.py:295
  24.5 12.2 %collective-permute-start.6 = (bf16[32,1024]{1,0:T(8,128)(2,1)S(1)}, bf16[32,1024]{1,0:T(8,128)(2,1)S(1)}, u32[]{:S(2)}, u32[]{:S(2)}) collective-permute-start(bf16[32,1024]{1,0:T(8,128)(2,1)S(1)} %get-tuple-element.27), channel_id=1, source_target_pairs={{0,128},{16,144},{32,160},{48,176},{64,192},{80,208},{96,224},{112... | collective-permute-start | bytes 196616 | tf_op jit(solution)/shard_map/ppermute | solution.py:295
  25.8 10.9 %collective-permute-start.7 = (bf16[32,1024]{1,0:T(8,128)(2,1)S(1)}, bf16[32,1024]{1,0:T(8,128)(2,1)S(1)}, u32[]{:S(2)}, u32[]{:S(2)}) collective-permute-start(bf16[32,1024]{1,0:T(8,128)(2,1)S(1)} %get-tuple-element.28), channel_id=1, source_target_pairs={{0,64},{16,80},{32,96},{48,112},{64,0},{80,16},{96,32},{112,48},{1... | collective-permute-start | bytes 196616 | tf_op jit(solution)/shard_map/ppermute | solution.py:295
  29.3 9.4 %collective-permute-start.11 = (bf16[16,1024]{1,0:T(8,128)(2,1)S(1)}, bf16[16,1024]{1,0:T(8,128)(2,1)S(1)}, u32[]{:S(2)}, u32[]{:S(2)}) collective-permute-start(bf16[16,1024]{1,0:T(8,128)(2,1)S(1)} %get-tuple-element.33), channel_id=1, source_target_pairs={{0,48},{16,32},{32,0},{48,16},{64,112},{80,96},{96,64},{112,80},{1... | collective-permute-start | bytes 98312 | tf_op jit(solution)/shard_map/ppermute | solution.py:299
  35.7 6.1 %collective-permute-start.12 = (bf16[16,1024]{1,0:T(8,128)(2,1)S(1)}, bf16[16,1024]{1,0:T(8,128)(2,1)S(1)}, u32[]{:S(2)}, u32[]{:S(2)}) collective-permute-start(bf16[16,1024]{1,0:T(8,128)(2,1)S(1)} %get-tuple-element.34), channel_id=1, source_target_pairs={{0,32},{16,48},{32,16},{48,0},{64,96},{80,112},{96,80},{112,64},{1... | collective-permute-start | bytes 98312 | tf_op jit(solution)/shard_map/ppermute | solution.py:299
  36.7 5.6 %collective-permute-start.8 = (bf16[16,1024]{1,0:T(8,128)(2,1)S(1)}, bf16[16,1024]{1,0:T(8,128)(2,1)S(1)}, u32[]{:S(2)}, u32[]{:S(2)}) collective-permute-start(bf16[16,1024]{1,0:T(8,128)(2,1)S(1)} %get-tuple-element.30), channel_id=1, source_target_pairs={{0,16},{16,0},{32,48},{48,32},{64,80},{80,64},{96,112},{112,96},{1... | collective-permute-start | bytes 98312 | tf_op jit(solution)/shard_map/ppermute | solution.py:299

commit v6 on v5

--- a/solution.py
+++ b/solution.py
@@ -300,7 +300,7 @@
 
     cross = over_y(cross, 3)
     three, one = add(0, home, cross, over_y(a1, 2), over_y(a3, 1))
-    mine, two = add(2 * ROWS, home, cross, over_y(b1, 2), over_y(b3, 1))
+    mine, two = add(2 * ROWS, home, cross, over_y(b3, 1), over_y(b1, 2))
     return total(mine, over_z(two, 2), over_z(three, 3), over_z(one, 1))
 
 

time: 43.1 us -> 42.7 us (level)
  the two profiles are of different devices: /device:TPU:24 before, /device:TPU:8 now
where the time goes in v6:
time: 42.7 us; the launch traced here: 42.2 us
  starting transfers between devices  22.9 us (54%)
  waiting for transfers between devices  9.84 us (23%)
  Pallas kernels  8.65 us (20%)
  between operations  0.74 us (2%)
    ppermute x3, starting transfers between devices, over_z(): return lax.ppermute(x, 'ckpt', pairs)  9.35 us
    ppermute x5, starting transfers between devices, shards(): lax.ppermute(x, 'ckpt', [(i, i ^ 4 * k) for i in range(16)])  7.23 us
    ppermute x3, starting transfers between devices, along(): lax.ppermute(parts[k], axis, [(i, shift(i, k)) for i in range(n)])  4.18 us
    pallas_call x1, Pallas kernels, scores(): pl.pallas_call(scores_kernel, out_shape=[jax.ShapeDtypeStruct((4 * ROWS,...  3.62 us
    ppermute x3, waiting for transfers between devices, over_z(): return lax.ppermute(x, 'ckpt', pairs)  3.58 us
    ppermute x3, waiting for transfers between devices, along(): lax.ppermute(parts[k], axis, [(i, shift(i, k)) for i in range(n)])  3.18 us
    pallas_call x1, Pallas kernels, factors(): pl.pallas_call(factors_kernel, out_shape=jax.ShapeDtypeStruct((rank + wid...  2.39 us
    ppermute x1, starting transfers between devices, shards(): near = lax.ppermute(own, 'corpus', [(i, i ^ 2) for i in range(16)])  2.01 us
  transfers between devices with their start and end apart: 13, of which 8 were waited for; matrix products, arithmetic and copies ran while one was open for 0% of the time, Pallas kernels for 5%

profile of v6, /device:TPU:8, one launch (start us, length us, event | category | flops | bytes accessed | tf_op | source)
XLA Modules:
  0.0 42.2 jit_solution(3436285290653790360)
XLA Ops:
  0.0 2.4 %factors.1 = bf16[128,128]{1,0:T(8,128)(2,1)S(1)} custom-call(bf16[128,4096]{1,0:T(8,128)(2,1)} %bitcast.17, bf16[128,4096]{1,0:T(8,128)(2,1)} %bitcast.18, bf16[64,4096]{1,0:T(8,128)(2,1)} %bitcast.19, bf16[64,4096]{1,0:T(8,128)(2,1)} %bitcast.20), custom_call_target="tpu_custom_call" | custom-call | tf_op jit(solution)/shard_map/factors/pallas_call | solution.py:60
  2.4 2.0 %collective-permute-start = (bf16[128,128]{1,0:T(8,128)(2,1)S(1)}, bf16[128,128]{1,0:T(8,128)(2,1)S(1)}, u32[]{:S(2)}, u32[]{:S(2)}) collective-permute-start(bf16[128,128]{1,0:T(8,128)(2,1)S(1)} %factors.1), channel_id=1, source_target_pairs={{0,2},{1,3},{2,0},{3,1},{4,6},{5,7},{6,4},{7,5},{8,10},{9,11},{10,... | collective-permute-start | bytes 98312 | tf_op jit(solution)/shard_map/ppermute | solution.py:284
  5.1 1.3 %collective-permute-done.after_hbm = bf16[128,128]{1,0:T(8,128)(2,1)S(1)} collective-permute-done((bf16[128,128]{1,0:T(8,128)(2,1)S(1)}, bf16[128,128]{1,0:T(8,128)(2,1)S(1)}, u32[]{:S(2)}, u32[]{:S(2)}) %collective-permute-start) | collective-permute-done | bytes 32800 | tf_op jit(solution)/shard_map/ppermute | solution.py:284
  6.4 2.8 %collective-permute-start.3 = (bf16[2,128,128]{2,1,0:T(8,128)(2,1)S(1)}, bf16[2,128,128]{2,1,0:T(8,128)(2,1)S(1)}, u32[]{:S(2)}, u32[]{:S(2)}) collective-permute-start(bf16[2,128,128]{2,1,0:T(8,128)(2,1)S(1)} %pad_maximum_fusion), channel_id=1, source_target_pairs={{0,12},{1,13},{2,14},{3,15},{4,8},{5,9},{6,10},{7,11},{8,4},{9,5},... | collective-permute-start | bytes 196616 | tf_op jit(solution)/shard_map/ppermute | solution.py:269
  9.3 0.8 %collective-permute-start.2 = (bf16[2,128,128]{2,1,0:T(8,128)(2,1)S(1)}, bf16[2,128,128]{2,1,0:T(8,128)(2,1)S(1)}, u32[]{:S(2)}, u32[]{:S(2)}) collective-permute-start(bf16[2,128,128]{2,1,0:T(8,128)(2,1)S(1)} %pad_maximum_fusion), channel_id=1, source_target_pairs={{0,8},{1,9},{2,10},{3,11},{4,12},{5,13},{6,14},{7,15},{8,0},{9,1},... | collective-permute-start | bytes 196616 | tf_op jit(solution)/shard_map/ppermute | solution.py:269
  10.1 0.5 %collective-permute-start.1 = (bf16[2,128,128]{2,1,0:T(8,128)(2,1)S(1)}, bf16[2,128,128]{2,1,0:T(8,128)(2,1)S(1)}, u32[]{:S(2)}, u32[]{:S(2)}) collective-permute-start(bf16[2,128,128]{2,1,0:T(8,128)(2,1)S(1)} %pad_maximum_fusion), channel_id=1, source_target_pairs={{0,4},{1,5},{2,6},{3,7},{4,0},{5,1},{6,2},{7,3},{8,12},{9,13},{10,... | collective-permute-start | bytes 196616 | tf_op jit(solution)/shard_map/ppermute | solution.py:269
  10.6 1.2 %choose.1 = (bf16[1024,1024]{1,0:T(8,128)(2,1)S(1)}, f32[8,128]{1,0:T(8,128)S(1)}, s32[16,128]{1,0:T(8,128)S(1)}) custom-call(s32[1]{0:T(128)S(6)} %copy.13.rate_ref, s32[1,1024]{1,0:T(1,128)} %bitcast.21, s32[16,128]{1,0:T(8,128)} %ids_hbm.1, bf16[128,128]{1,0:T(8,128)(2,1)S(1)} %collective-permute-done.after_hbm), custom_call_target="tpu_custom_call" | custom-call | flops 10000000000 | bytes 2097152 | tf_op jit(solution)/shard_map/choose/pallas_call | solution.py:135
  11.8 2.5 %collective-permute-done.1 = bf16[2,128,128]{2,1,0:T(8,128)(2,1)S(1)} collective-permute-done((bf16[2,128,128]{2,1,0:T(8,128)(2,1)S(1)}, bf16[2,128,128]{2,1,0:T(8,128)(2,1)S(1)}, u32[]{:S(2)}, u32[]{:S(2)}) %collective-permute-start.1) | collective-permute-done | bytes 65568 | tf_op jit(solution)/shard_map/ppermute | solution.py:269
  14.3 0.7 %collective-permute-done.2 = bf16[2,128,128]{2,1,0:T(8,128)(2,1)S(1)} collective-permute-done((bf16[2,128,128]{2,1,0:T(8,128)(2,1)S(1)}, bf16[2,128,128]{2,1,0:T(8,128)(2,1)S(1)}, u32[]{:S(2)}, u32[]{:S(2)}) %collective-permute-start.2) | collective-permute-done | bytes 65568 | tf_op jit(solution)/shard_map/ppermute | solution.py:269
  15.2 0.7 %near_grads.1.near_ref = bf16[128,4096]{1,0:T(8,128)(2,1)S(1)} custom-call(s32[16,128]{1,0:T(8,128)S(1)} %get-tuple-element.20.ids_ref, bf16[8,128,128]{2,1,0:T(8,128)(2,1)S(1)} %constant_dynamic-update-slice_fusion.mine_ref), custom_call_target="tpu_custom_call" | custom-call | flops 1000000000 | bytes 2097152 | tf_op jit(solution)/shard_map/near_grads/pallas_call | solution.py:164
  15.9 0.8 %collective-permute-done.4.other_ref = bf16[8,128,128]{2,1,0:T(8,128)(2,1)S(1)} collective-permute-done((bf16[8,128,128]{2,1,0:T(8,128)(2,1)S(1)}, bf16[8,128,128]{2,1,0:T(8,128)(2,1)S(1)}, u32[]{:S(2)}, u32[]{:S(2)}) %collective-permute-start.4) | collective-permute-done | bytes 262176 | tf_op jit(solution)/shard_map/ppermute | solution.py:291
  16.7 3.6 %scores.1 = (bf16[64,1024]{1,0:T(8,128)(2,1)S(1)}, bf16[64,1024]{1,0:T(8,128)(2,1)S(1)}, bf16[32,1024]{1,0:T(8,128)(2,1)S(1)}, bf16[32,1024]{1,0:T(8,128)(2,1)S(...) custom-call(s32[16,128]{1,0:T(8,128)S(1)} %get-tuple-element.20.ids_ref, ...), custom_call_target="tpu_custom_call" | custom-call | tf_op jit(solution)/shard_map/scores/pallas_call | solution.py:213
  20.3 1.7 %collective-permute-start.5 = (bf16[64,1024]{1,0:T(8,128)(2,1)S(1)}, bf16[64,1024]{1,0:T(8,128)(2,1)S(1)}, u32[]{:S(2)}, u32[]{:S(2)}) collective-permute-start(bf16[64,1024]{1,0:T(8,128)(2,1)S(1)} %get-tuple-element.26), channel_id=1, source_target_pairs={{0,192},{16,208},{32,224},{48,240},{64,128},{80,144},{96,160},{112... | collective-permute-start | bytes 393224 | tf_op jit(solution)/shard_map/ppermute | solution.py:295
  22.0 1.2 %collective-permute-start.9 = (bf16[32,1024]{1,0:T(8,128)(2,1)S(1)}, bf16[32,1024]{1,0:T(8,128)(2,1)S(1)}, u32[]{:S(2)}, u32[]{:S(2)}) collective-permute-start(bf16[32,1024]{1,0:T(8,128)(2,1)S(1)} %get-tuple-element.31), channel_id=1, source_target_pairs={{0,128},{16,144},{32,160},{48,176},{64,192},{80,208},{96,224},{112... | collective-permute-start | bytes 196616 | tf_op jit(solution)/shard_map/ppermute | solution.py:295
  23.2 1.3 %collective-permute-start.10 = (bf16[32,1024]{1,0:T(8,128)(2,1)S(1)}, bf16[32,1024]{1,0:T(8,128)(2,1)S(1)}, u32[]{:S(2)}, u32[]{:S(2)}) collective-permute-start(bf16[32,1024]{1,0:T(8,128)(2,1)S(1)} %get-tuple-element.32), channel_id=1, source_target_pairs={{0,64},{16,80},{32,96},{48,112},{64,0},{80,16},{96,32},{112,48},{1... | collective-permute-start | bytes 196616 | tf_op jit(solution)/shard_map/ppermute | solution.py:295
  24.5 0.7 %collective-permute-start.6 = (bf16[32,1024]{1,0:T(8,128)(2,1)S(1)}, bf16[32,1024]{1,0:T(8,128)(2,1)S(1)}, u32[]{:S(2)}, u32[]{:S(2)}) collective-permute-start(bf16[32,1024]{1,0:T(8,128)(2,1)S(1)} %get-tuple-element.27), channel_id=1, source_target_pairs={{0,64},{16,80},{32,96},{48,112},{64,0},{80,16},{96,32},{112,48},{1... | collective-permute-start | bytes 196616 | tf_op jit(solution)/shard_map/ppermute | solution.py:295
  25.2 2.3 %collective-permute-start.7 = (bf16[32,1024]{1,0:T(8,128)(2,1)S(1)}, bf16[32,1024]{1,0:T(8,128)(2,1)S(1)}, u32[]{:S(2)}, u32[]{:S(2)}) collective-permute-start(bf16[32,1024]{1,0:T(8,128)(2,1)S(1)} %get-tuple-element.28), channel_id=1, source_target_pairs={{0,128},{16,144},{32,160},{48,176},{64,192},{80,208},{96,224},{112... | collective-permute-start | bytes 196616 | tf_op jit(solution)/shard_map/ppermute | solution.py:295
  27.6 0.9 %collective-permute-done.9.refs_2_ = bf16[32,1024]{1,0:T(8,128)(2,1)S(1)} collective-permute-done((bf16[32,1024]{1,0:T(8,128)(2,1)S(1)}, bf16[32,1024]{1,0:T(8,128)(2,1)S(1)}, u32[]{:S(2)}, u32[]{:S(2)}) %collective-permute-start.9) | collective-permute-done | bytes 65568 | tf_op jit(solution)/shard_map/ppermute | solution.py:295
  28.5 6.4 %collective-permute-start.11 = (bf16[16,1024]{1,0:T(8,128)(2,1)S(1)}, bf16[16,1024]{1,0:T(8,128)(2,1)S(1)}, u32[]{:S(2)}, u32[]{:S(2)}) collective-permute-start(bf16[16,1024]{1,0:T(8,128)(2,1)S(1)} %get-tuple-element.33), channel_id=1, source_target_pairs={{0,48},{16,32},{32,0},{48,16},{64,112},{80,96},{96,64},{112,80},{1... | collective-permute-start | bytes 98312 | tf_op jit(solution)/shard_map/ppermute | solution.py:299
  34.9 1.0 %collective-permute-start.12 = (bf16[16,1024]{1,0:T(8,128)(2,1)S(1)}, bf16[16,1024]{1,0:T(8,128)(2,1)S(1)}, u32[]{:S(2)}, u32[]{:S(2)}) collective-permute-start(bf16[16,1024]{1,0:T(8,128)(2,1)S(1)} %get-tuple-element.34), channel_id=1, source_target_pairs={{0,32},{16,48},{32,16},{48,0},{64,96},{80,112},{96,80},{112,64},{1... | collective-permute-start | bytes 98312 | tf_op jit(solution)/shard_map/ppermute | solution.py:299
  35.9 2.0 %collective-permute-start.8 = (bf16[16,1024]{1,0:T(8,128)(2,1)S(1)}, bf16[16,1024]{1,0:T(8,128)(2,1)S(1)}, u32[]{:S(2)}, u32[]{:S(2)}) collective-permute-start(bf16[16,1024]{1,0:T(8,128)(2,1)S(1)} %get-tuple-element.30), channel_id=1, source_target_pairs={{0,16},{16,0},{32,48},{48,32},{64,80},{80,64},{96,112},{112,96},{1... | collective-permute-start | bytes 98312 | tf_op jit(solution)/shard_map/ppermute | solution.py:299
  38.1 2.8 %collective-permute-done.12.d = bf16[16,1024]{1,0:T(8,128)(2,1)S(1)} collective-permute-done((bf16[16,1024]{1,0:T(8,128)(2,1)S(1)}, bf16[16,1024]{1,0:T(8,128)(2,1)S(1)}, u32[]{:S(2)}, u32[]{:S(2)}) %collective-permute-start.12) | collective-permute-done | bytes 32800 | tf_op jit(solution)/shard_map/ppermute | solution.py:299
  40.9 0.6 %collective-permute-done.8.b = bf16[16,1024]{1,0:T(8,128)(2,1)S(1)} collective-permute-done((bf16[16,1024]{1,0:T(8,128)(2,1)S(1)}, bf16[16,1024]{1,0:T(8,128)(2,1)S(1)}, u32[]{:S(2)}, u32[]{:S(2)}) %collective-permute-start.8) | collective-permute-done | bytes 32800 | tf_op jit(solution)/shard_map/ppermute | solution.py:299
  41.5 0.6 %total.1 = f32[16,1024]{1,0:T(8,128)} custom-call(f32[16,1024]{1,0:T(8,128)S(1)} %get-tuple-element.29.a, bf16[16,1024]{1,0:T(8,128)(2,1)S(1)} %collective-permute-done.8.b, bf16[16,1024]{1,0:T(8,128)(2,1)S(1)} %collective-permute-done.11.c, bf16[16,1024]{1,0:T(8,128)(2,1)S(1)} %collective-permute-done.12.d), custom_call_target="tpu_custom_call" | custom-call | tf_op jit(solution)/shard_map/total/pallas_call | solution.py:256
  (20 shorter events, 0.4 us)
Async XLA Ops:
  2.4 4.0 %collective-permute-start = (bf16[128,128]{1,0:T(8,128)(2,1)S(1)}, bf16[128,128]{1,0:T(8,128)(2,1)S(1)}, u32[]{:S(2)}, u32[]{:S(2)}) collective-permute-start(bf16[128,128]{1,0:T(8,128)(2,1)S(1)} %factors.1), channel_id=1, source_target_pairs={{0,2},{1,3},{2,0},{3,1},{4,6},{5,7},{6,4},{7,5},{8,10},{9,11},{10,... | collective-permute-start | bytes 98312 | tf_op jit(solution)/shard_map/ppermute | solution.py:284
  6.4 8.6 %collective-permute-start.3 = (bf16[2,128,128]{2,1,0:T(8,128)(2,1)S(1)}, bf16[2,128,128]{2,1,0:T(8,128)(2,1)S(1)}, u32[]{:S(2)}, u32[]{:S(2)}) collective-permute-start(bf16[2,128,128]{2,1,0:T(8,128)(2,1)S(1)} %pad_maximum_fusion), channel_id=1, source_target_pairs={{0,12},{1,13},{2,14},{3,15},{4,8},{5,9},{6,10},{7,11},{8,4},{9,5},... | collective-permute-start | bytes 196616 | tf_op jit(solution)/shard_map/ppermute | solution.py:269
  9.3 5.8 %collective-permute-start.2 = (bf16[2,128,128]{2,1,0:T(8,128)(2,1)S(1)}, bf16[2,128,128]{2,1,0:T(8,128)(2,1)S(1)}, u32[]{:S(2)}, u32[]{:S(2)}) collective-permute-start(bf16[2,128,128]{2,1,0:T(8,128)(2,1)S(1)} %pad_maximum_fusion), channel_id=1, source_target_pairs={{0,8},{1,9},{2,10},{3,11},{4,12},{5,13},{6,14},{7,15},{8,0},{9,1},... | collective-permute-start | bytes 196616 | tf_op jit(solution)/shard_map/ppermute | solution.py:269
  10.1 4.3 %collective-permute-start.1 = (bf16[2,128,128]{2,1,0:T(8,128)(2,1)S(1)}, bf16[2,128,128]{2,1,0:T(8,128)(2,1)S(1)}, u32[]{:S(2)}, u32[]{:S(2)}) collective-permute-start(bf16[2,128,128]{2,1,0:T(8,128)(2,1)S(1)} %pad_maximum_fusion), channel_id=1, source_target_pairs={{0,4},{1,5},{2,6},{3,7},{4,0},{5,1},{6,2},{7,3},{8,12},{9,13},{10,... | collective-permute-start | bytes 196616 | tf_op jit(solution)/shard_map/ppermute | solution.py:269
  10.6 6.1 %slice-start = ((s8[8388608]{0:T(1024)(128)(4,1)}), s8[4194304]{0:T(1024)(128)(4,1)S(1)}, s32[]{:S(2)}) async-start(s8[8388608]{0:T(1024)(128)(4,1)} %bitcast.12), calls=%async_computation | async-start | bytes 8388608
  10.6 6.1 %slice-start.1 = ((s8[8388608]{0:T(1024)(128)(4,1)}), s8[4194304]{0:T(1024)(128)(4,1)S(1)}, s32[]{:S(2)}) async-start(s8[8388608]{0:T(1024)(128)(4,1)} %bitcast.12), calls=%async_computation.1 | async-start | bytes 8388608
  15.1 1.6 %collective-permute-start.4 = (bf16[8,128,128]{2,1,0:T(8,128)(2,1)S(1)}, bf16[8,128,128]{2,1,0:T(8,128)(2,1)S(1)}, u32[]{:S(2)}, u32[]{:S(2)}) collective-permute-start(bf16[8,128,128]{2,1,0:T(8,128)(2,1)S(1)} %constant_dynamic-update-slice_fusion.mine_ref), channel_id=1, source_target_pairs={{0,1},{1,0},{2,3},{3,2},{4,5},{5,4},{6,7},{7,6},{8,9},{9,8},{10,11... | collective-permute-start | bytes 786440 | tf_op jit(solution)/shard_map/ppermute | solution.py:291
  20.3 8.2 %collective-permute-start.5 = (bf16[64,1024]{1,0:T(8,128)(2,1)S(1)}, bf16[64,1024]{1,0:T(8,128)(2,1)S(1)}, u32[]{:S(2)}, u32[]{:S(2)}) collective-permute-start(bf16[64,1024]{1,0:T(8,128)(2,1)S(1)} %get-tuple-element.26), channel_id=1, source_target_pairs={{0,192},{16,208},{32,224},{48,240},{64,128},{80,144},{96,160},{112... | collective-permute-start | bytes 393224 | tf_op jit(solution)/shard_map/ppermute | solution.py:295
  22.0 6.5 %collective-permute-start.9 = (bf16[32,1024]{1,0:T(8,128)(2,1)S(1)}, bf16[32,1024]{1,0:T(8,128)(2,1)S(1)}, u32[]{:S(2)}, u32[]{:S(2)}) collective-permute-start(bf16[32,1024]{1,0:T(8,128)(2,1)S(1)} %get-tuple-element.31), channel_id=1, source_target_pairs={{0,128},{16,144},{32,160},{48,176},{64,192},{80,208},{96,224},{112... | collective-permute-start | bytes 196616 | tf_op jit(solution)/shard_map/ppermute | solution.py:295
  23.2 5.3 %collective-permute-start.10 = (bf16[32,1024]{1,0:T(8,128)(2,1)S(1)}, bf16[32,1024]{1,0:T(8,128)(2,1)S(1)}, u32[]{:S(2)}, u32[]{:S(2)}) collective-permute-start(bf16[32,1024]{1,0:T(8,128)(2,1)S(1)} %get-tuple-element.32), channel_id=1, source_target_pairs={{0,64},{16,80},{32,96},{48,112},{64,0},{80,16},{96,32},{112,48},{1... | collective-permute-start | bytes 196616 | tf_op jit(solution)/shard_map/ppermute | solution.py:295
  24.5 11.4 %collective-permute-start.6 = (bf16[32,1024]{1,0:T(8,128)(2,1)S(1)}, bf16[32,1024]{1,0:T(8,128)(2,1)S(1)}, u32[]{:S(2)}, u32[]{:S(2)}) collective-permute-start(bf16[32,1024]{1,0:T(8,128)(2,1)S(1)} %get-tuple-element.27), channel_id=1, source_target_pairs={{0,64},{16,80},{32,96},{48,112},{64,0},{80,16},{96,32},{112,48},{1... | collective-permute-start | bytes 196616 | tf_op jit(solution)/shard_map/ppermute | solution.py:295
  25.2 10.6 %collective-permute-start.7 = (bf16[32,1024]{1,0:T(8,128)(2,1)S(1)}, bf16[32,1024]{1,0:T(8,128)(2,1)S(1)}, u32[]{:S(2)}, u32[]{:S(2)}) collective-permute-start(bf16[32,1024]{1,0:T(8,128)(2,1)S(1)} %get-tuple-element.28), channel_id=1, source_target_pairs={{0,128},{16,144},{32,160},{48,176},{64,192},{80,208},{96,224},{112... | collective-permute-start | bytes 196616 | tf_op jit(solution)/shard_map/ppermute | solution.py:295
  28.5 9.6 %collective-permute-start.11 = (bf16[16,1024]{1,0:T(8,128)(2,1)S(1)}, bf16[16,1024]{1,0:T(8,128)(2,1)S(1)}, u32[]{:S(2)}, u32[]{:S(2)}) collective-permute-start(bf16[16,1024]{1,0:T(8,128)(2,1)S(1)} %get-tuple-element.33), channel_id=1, source_target_pairs={{0,48},{16,32},{32,0},{48,16},{64,112},{80,96},{96,64},{112,80},{1... | collective-permute-start | bytes 98312 | tf_op jit(solution)/shard_map/ppermute | solution.py:299
  34.9 6.0 %collective-permute-start.12 = (bf16[16,1024]{1,0:T(8,128)(2,1)S(1)}, bf16[16,1024]{1,0:T(8,128)(2,1)S(1)}, u32[]{:S(2)}, u32[]{:S(2)}) collective-permute-start(bf16[16,1024]{1,0:T(8,128)(2,1)S(1)} %get-tuple-element.34), channel_id=1, source_target_pairs={{0,32},{16,48},{32,16},{48,0},{64,96},{80,112},{96,80},{112,64},{1... | collective-permute-start | bytes 98312 | tf_op jit(solution)/shard_map/ppermute | solution.py:299
  35.9 5.6 %collective-permute-start.8 = (bf16[16,1024]{1,0:T(8,128)(2,1)S(1)}, bf16[16,1024]{1,0:T(8,128)(2,1)S(1)}, u32[]{:S(2)}, u32[]{:S(2)}) collective-permute-start(bf16[16,1024]{1,0:T(8,128)(2,1)S(1)} %get-tuple-element.30), channel_id=1, source_target_pairs={{0,16},{16,0},{32,48},{48,32},{64,80},{80,64},{96,112},{112,96},{1... | collective-permute-start | bytes 98312 | tf_op jit(solution)/shard_map/ppermute | solution.py:299
